TPU v7x, 32 devices: a whole 2x2x4 slice. The times are simulated.
32 devices in a mesh: paths: 16 (over z, x, core), trades: 2 (over y).
Axes of the slice: x: 2, y: 2, z: 4, core: 2. Of those that a mesh axis runs over, the one named last changes fastest.
Arguments:
- basis: bfloat16 [16384, 512], P('paths'), may hold values from -6 to 6
- coef: bfloat16 [512, 4096], P('paths', 'trades'), may hold values from -0.25 to 0.25
- membership: int32 [4096, 512], P('trades'), may hold values from -1 to 1, as said below
- counts: int32 [512], replicated, may hold values from 1 to 15, as said below
- borrow: float32 [512], replicated, may hold values from 0.3 to 3
- lend: float32 [512], replicated, may hold values from 0.3 to 3
Outputs:
- d_basis: float32 [16384, 512], P(('paths', 'trades'))
- d_coef: float32 [512, 4096], P('paths', 'trades')
Inputs may be any that keep to these rules, and one draw needn't show every extreme that they name: Each row of membership has exactly one nonzero entry, 1 or -1, and every set holds at least one trade. counts[s] is the number of nonzero entries in column s of membership; some set holds exactly one trade and some set exactly 15.
All inputs are finite; a program needn't handle non-finite values.
Results may differ from a plain program's by a relative error of at most 0.0042.
Values may be sent and summed in bfloat16 or wider, within the bound.
A program may use at most 64 MiB of HBM per device.

v0:
```python
import jax
import jax.numpy as jnp
from jax import lax
from jax.sharding import PartitionSpec as P


def funding(netted, scale, borrow, lend):
    scaled = netted * scale
    grad = (borrow * jax.nn.sigmoid(scaled) + lend * jax.nn.sigmoid(-scaled)) * scale
    return grad.astype(jnp.bfloat16)


def body(basis, coef, membership, counts, borrow, lend):
    path_rows = basis.shape[0]
    member = membership.astype(jnp.bfloat16)
    coef_full = lax.all_gather(coef, "paths", axis=0, tiled=True)
    trade_value = jnp.dot(basis, coef_full, preferred_element_type=jnp.float32)
    exposure = jax.nn.softplus(trade_value).astype(jnp.bfloat16)
    partial_net = jnp.dot(exposure, member, preferred_element_type=jnp.float32)
    scale_all = lax.rsqrt(counts.astype(jnp.float32))
    net_share = lax.psum_scatter(partial_net, "trades", scatter_dimension=1, tiled=True)
    width_sets = net_share.shape[1]
    offset_sets = lax.axis_index("trades") * width_sets
    grad_share = funding(
        net_share,
        lax.dynamic_slice_in_dim(scale_all, offset_sets, width_sets, 0),
        lax.dynamic_slice_in_dim(borrow, offset_sets, width_sets, 0),
        lax.dynamic_slice_in_dim(lend, offset_sets, width_sets, 0),
    )
    set_grad = lax.all_gather(grad_share, "trades", axis=1, tiled=True)
    trade_grad = lax.dot_general(
        set_grad, member, (((1,), (1,)), ((), ())), preferred_element_type=jnp.float32
    )
    value_grad = (trade_grad * jax.nn.sigmoid(trade_value)).astype(jnp.bfloat16)
    d_basis = lax.psum_scatter(
        lax.dot_general(
            value_grad, coef_full, (((1,), (1,)), ((), ())), preferred_element_type=jnp.float32
        ),
        "trades",
        scatter_dimension=0,
        tiled=True,
    )
    factor = 1.0 / jnp.sqrt(jnp.float32(path_rows * lax.axis_size("paths")))
    product = lax.dot_general(
        basis, value_grad, (((0,), (0,)), ((), ())), preferred_element_type=jnp.float32
    )
    d_coef = lax.psum_scatter(product * factor, "paths", scatter_dimension=0, tiled=True)
    return (d_basis, d_coef)


def solution(mesh):
    placed = (P("paths", None), P("paths", "trades"), P("trades", None), P(), P(), P())
    return jax.shard_map(
        body,
        mesh=mesh,
        in_specs=placed,
        out_specs=(P(("paths", "trades"), None), P("paths", "trades")),
        check_vma=False,
    )
```

profile of v0, /device:TPU:0, one launch (start us, length us, event | category | flops | bytes accessed | tf_op | source)
XLA Modules:
  0.0 251.3 jit_solution(966986870016290100)
XLA Ops:
  7.2 0.0 copy-start
  7.2 0.0 all-gather.3.cloned.1.call-start
  7.2 0.7 all-gather.3.cloned.1.call-update
  7.9 0.0 reduce-scatter.6.cloned.1.call-start
  8.0 46.3 %all-gather.3.cloned.1.call-done = bf16[512,2048]{1,0:T(8,128)(2,1)} async-done(((bf16[32,2048]{1,0:T(8,128)(2,1)}), bf16[512,2048]{1,0:T(8,128)(2,1)}) %all-gather.3.cloned.1.call-update) | async-done | bytes 2097168 | tf_op jit(solution)/shard_map/all_gather | solution.py:16
  54.3 0.0 copy-done
  54.3 0.0 copy-start.4
  54.3 4.1 %fusion.6 = f32[1024,2048]{1,0:T(8,128)S(1)} fusion(bf16[1024,512]{1,0:T(8,128)(2,1)S(1)} %copy-done, bf16[512,2048]{1,0:T(8,128)(2,1)} %all-gather.3.cloned.1.call-done), kind=kOutput, calls=%fused_computation.10 | convolution fusion | flops 2147483648 | bytes 11534336 | tf_op jit(solution)/shard_map/dot_general | solution.py:17
  58.4 0.0 copy-start.6
  58.4 3.2 %copy-done.6 = f32[1024,2048]{1,0:T(8,128)} copy-done((f32[1024,2048]{1,0:T(8,128)}, f32[1024,2048]{1,0:T(8,128)S(1)}, u32[]{:S(2)}) %copy-start.6) | copy-done | bytes 8388632
  61.6 0.0 copy-done.4
  61.6 0.0 copy-start.2
  61.6 0.0 copy-start.3
  61.6 0.0 copy-start.1
  61.6 6.2 %fusion.1 = f32[1024,512]{1,0:T(8,128)} fusion(f32[1024,2048]{1,0:T(8,128)S(1)} %fusion.6, s32[2048,512]{1,0:T(8,128)S(1)} %copy-done.4), kind=kOutput, calls=%fused_computation.4 | convolution fusion | flops 2163212288 | bytes 14680064 | tf_op jit(solution)/shard_map/dot_general | solution.py:19
  67.8 0.0 reduce-scatter.6.cloned.1.call-update
  67.9 0.0 all-gather.5.cloned.1.call-start
  67.9 0.0 copy-done.2
  67.9 0.1 dynamic_slice.9
  68.0 0.0 copy-done.3
  68.0 0.1 dynamic_slice.11
  68.1 0.0 copy-done.1
  68.1 0.1 dynamic_slice.10
  68.2 30.5 %reduce-scatter.6.cloned.1.call-done = f32[1024,256]{1,0:T(8,128)} async-done(((f32[1024,512]{1,0:T(8,128)}), f32[1024,256]{1,0:T(8,128)}) %reduce-scatter.6.cloned.1.call-update) | async-done | bytes 1048592 | tf_op jit(solution)/shard_map/reduce_scatter | solution.py:21
  98.6 2.6 %multiply_convert_fusion.1 = bf16[1024,256]{1,0:T(8,128)(2,1)} fusion(f32[1024,256]{1,0:T(8,128)} %reduce-scatter.6.cloned.1.call-done, f32[256]{0:T(256)S(1)} %dynamic_slice.11, f32[256]{0:T(256)S(1)} %dynamic_slice.10, f32[256]{0:T(256)S(1)} %dynamic_slice.9), kind=kLoop, calls=%fused_computation.5 | loop fusion | flops 2883584 | bytes 1575936 | tf_op jit(solution)/shard_map/convert_element_type | solution.py:10
  101.2 0.0 all-gather.5.cloned.1.call-update
  101.2 0.0 copy-start.5
  101.2 0.0 reduce-scatter.8.cloned.1.call-start
  101.3 21.4 %all-gather.5.cloned.1.call-done = bf16[1024,512]{1,0:T(8,128)(2,1)} async-done(((bf16[1024,256]{1,0:T(8,128)(2,1)}), bf16[1024,512]{1,0:T(8,128)(2,1)}) %all-gather.5.cloned.1.call-update) | async-done | bytes 1048592 | tf_op jit(solution)/shard_map/all_gather | solution.py:30
  122.7 7.8 %multiply_convert_fusion = bf16[1024,2048]{1,0:T(8,128)(2,1)S(1)} fusion(f32[1024,2048]{1,0:T(8,128)} %copy-done.6, bf16[1024,512]{1,0:T(8,128)(2,1)} %all-gather.5.cloned.1.call-done, s32[2048,512]{1,0:T(8,128)} %param.8), kind=kOutput, calls=%fused_computation.2 | convolution fusion | flops 2159017984 | bytes 17825792 | tf_op jit(solution)/shard_map/dot_general | solution.py:31
  130.5 0.0 copy-start.7
  130.5 1.9 copy-done.7
  132.4 0.0 copy-done.5
  132.4 3.7 %fusion.7 = f32[1024,512]{1,0:T(8,128)} fusion(bf16[1024,2048]{1,0:T(8,128)(2,1)S(1)} %multiply_convert_fusion, bf16[512,2048]{1,0:T(8,128)(2,1)S(1)} %copy-done.5), kind=kOutput, calls=%fused_computation.11 | convolution fusion | flops 2147483648 | bytes 8388608 | tf_op jit(solution)/shard_map/dot_general | solution.py:36
  136.1 0.0 reduce-scatter.8.cloned.1.call-update
  136.2 0.2 reduce-scatter.10.cloned.1.call-start
  136.4 6.7 %multiply_bitcast_fusion = f32[512,2048]{0,1:T(8,128)} fusion(bf16[1024,2048]{1,0:T(8,128)(2,1)} %copy-done.7, bf16[1024,512]{1,0:T(8,128)(2,1)S(1)} %copy-done), kind=kOutput, calls=%fused_computation.3 | convolution fusion | flops 2148532224 | bytes 9437184 | tf_op jit(solution)/shard_map/dot_general | solution.py:44
  143.1 5.4 %copy.10 = f32[512,2048]{1,0:T(8,128)} copy(f32[512,2048]{0,1:T(8,128)} %multiply_bitcast_fusion) | data formatting | bytes 8388608
  148.4 0.0 reduce-scatter.10.cloned.1.call-update
  148.5 19.7 %reduce-scatter.8.cloned.1.call-done = f32[512,512]{1,0:T(8,128)} async-done(((f32[1024,512]{1,0:T(8,128)}), f32[512,512]{1,0:T(8,128)}) %reduce-scatter.8.cloned.1.call-update) | async-done | bytes 1048592 | tf_op jit(solution)/shard_map/reduce_scatter | solution.py:35
  168.2 76.6 %reduce-scatter.10.cloned.1.call-done = f32[32,2048]{1,0:T(8,128)} async-done(((f32[512,2048]{1,0:T(8,128)}), f32[32,2048]{1,0:T(8,128)}) %reduce-scatter.10.cloned.1.call-update) | async-done | bytes 262160
  (1 shorter events, 0.0 us)
Async XLA Ops:
  7.2 47.1 %copy-start = (bf16[1024,512]{1,0:T(8,128)(2,1)S(1)}, bf16[1024,512]{1,0:T(8,128)(2,1)}, u32[]{:S(2)}) copy-start(bf16[1024,512]{1,0:T(8,128)(2,1)} %param.6) | copy-start | bytes 3145732
  7.2 47.1 %all-gather.3.cloned.1.call-start = ((), (), s32[]{:S(2)}) async-start(), calls=%async_computation.3 | async-start | bytes 2228224 | tf_op jit(solution)/shard_map/all_gather | solution.py:16
  7.9 90.7 %reduce-scatter.6.cloned.1.call-start = ((), (), s32[]{:S(2)}) async-start(), calls=%async_computation.4 | async-start | bytes 3145728 | tf_op jit(solution)/shard_map/reduce_scatter | solution.py:21
  54.3 7.3 %copy-start.4 = (s32[2048,512]{1,0:T(8,128)S(1)}, s32[2048,512]{1,0:T(8,128)}, u32[]{:S(2)}) copy-start(s32[2048,512]{1,0:T(8,128)} %param.8) | copy-start | bytes 12582916
  58.4 3.2 %copy-start.6 = (f32[1024,2048]{1,0:T(8,128)}, f32[1024,2048]{1,0:T(8,128)S(1)}, u32[]{:S(2)}) copy-start(f32[1024,2048]{1,0:T(8,128)S(1)} %fusion.6) | copy-start | bytes 25165828
  61.6 6.3 %copy-start.2 = (f32[512]{0:T(512)S(1)}, f32[512]{0:T(512)}, u32[]{:S(2)}) copy-start(f32[512]{0:T(512)} %param.10) | copy-start | bytes 6148
  61.6 6.4 %copy-start.3 = (f32[512]{0:T(512)S(1)}, f32[512]{0:T(512)}, u32[]{:S(2)}) copy-start(f32[512]{0:T(512)} %param.11) | copy-start | bytes 6148
  61.6 6.5 %copy-start.1 = (s32[512]{0:T(512)S(1)}, s32[512]{0:T(512)}, u32[]{:S(2)}) copy-start(s32[512]{0:T(512)} %param.9) | copy-start | bytes 6148
  67.9 54.8 %all-gather.5.cloned.1.call-start = ((), (), s32[]{:S(2)}) async-start(), calls=%async_computation.5 | async-start | bytes 1572864 | tf_op jit(solution)/shard_map/all_gather | solution.py:30
  101.2 31.2 %copy-start.5 = (bf16[512,2048]{1,0:T(8,128)(2,1)S(1)}, bf16[512,2048]{1,0:T(8,128)(2,1)}, u32[]{:S(2)}) copy-start(bf16[512,2048]{1,0:T(8,128)(2,1)} %all-gather.3.cloned.1.call-done) | copy-start | bytes 6291460
  101.2 66.9 %reduce-scatter.8.cloned.1.call-start = ((), (), s32[]{:S(2)}) async-start(), calls=%async_computation.6 | async-start | bytes 3145728 | tf_op jit(solution)/shard_map/reduce_scatter | solution.py:35
  130.5 1.9 copy-start.7
  136.2 108.6 %reduce-scatter.10.cloned.1.call-start = ((), (), s32[]{:S(2)}) async-start(), calls=%async_computation.7 | async-start | bytes 4456448
Sparse Core Ops, SparseCore 0:
  10.2 44.0 all-gather.2
  68.0 30.6 reduce-scatter.5
  101.4 21.2 all-gather.4
  136.3 31.8 reduce-scatter.7
  172.4 72.3 reduce-scatter.9
where the time goes:
time: 252 us; the launch traced here: 251 us
  waiting for transfers between devices  195 us (77%)
  matrix products  28.5 us (11%)
  between operations  13.8 us (5%)
  local copies, waits for them, and re-layouts  10.8 us (4%)
  other arithmetic  2.58 us (1%)
    unnamed x6, waiting for transfers between devices  77.4 us
    all_gather x1, waiting for transfers between devices, body(): coef_full = lax.all_gather(coef, 'paths', axis=0, tiled=True)  46.3 us
    reduce_scatter x1, waiting for transfers between devices, body(): lax.psum_scatter(partial_net, 'trades', scatter_dimension=1, tiled=True)  30.5 us
    all_gather x1, waiting for transfers between devices, body(): set_grad = lax.all_gather(grad_share, 'trades', axis=1, tiled=True)  21.4 us
    reduce_scatter x1, waiting for transfers between devices, body(): lax.psum_scatter(lax.dot_general(value_grad, coef_full, (((1,), (1,)), ((...  19.7 us
    unnamed x17, local copies, waits for them, and re-layouts  10.6 us
    dot_general x1, matrix products, body(): lax.dot_general(set_grad, member, (((1,), (1,)), ((), ())), preferred_ele...  7.79 us
    dot_general x1, matrix products, body(): lax.dot_general(basis, value_grad, (((0,), (0,)), ((), ())), preferred_el...  6.67 us
  transfers between devices with their start and end apart: 5, of which 5 were waited for; matrix products, arithmetic and copies ran while one was open for 5% of the time, Pallas kernels for 0%

commit v1 on v0

--- a/solution.py
+++ b/solution.py
@@ -1,7 +1,233 @@
+import functools
+
 import jax
 import jax.numpy as jnp
 from jax import lax
+from jax.experimental import pallas as pl
+from jax.experimental.pallas import tpu as pltpu
 from jax.sharding import PartitionSpec as P
+
+MESH = pl.DeviceIdType.MESH
+VMEM = pl.BlockSpec(memory_space=pltpu.VMEM)
+
+
+def place():
+    p, y = lax.axis_index("paths"), lax.axis_index("trades")
+    return p // 4, lax.rem(p // 2, 2), lax.rem(p, 2), y
+
+
+def device(z, x, c, y):
+    return (z * 4 + x * 2 + c, y)
+
+
+def greet(z, x, c, y):
+    barrier = pltpu.get_barrier_semaphore()
+    others = [device(lax.rem(z + k, 4), x, c, y) for k in (1, 2, 3)]
+    others += [device(z, 1 - x, c, y), device(z, x, 1 - c, y), device(z, x, c, 1 - y)]
+    for other in others:
+        pl.semaphore_signal(barrier, inc=1, device_id=other, device_id_type=MESH)
+    pl.semaphore_wait(barrier, len(others))
+
+
+def remote(src, dst, sems, i, target):
+    return pltpu.make_async_remote_copy(
+        src_ref=src,
+        dst_ref=dst,
+        send_sem=sems[0].at[i],
+        recv_sem=sems[1].at[i],
+        device_id=target,
+        device_id_type=MESH,
+    )
+
+
+def gather_kernel(coef_ref, idx_ref, full_ref, idxo_ref, *sems):
+    zs, xas, yas, xbs, ybs, cs, ids = [sems[2 * i : 2 * i + 2] for i in range(7)]
+    z, x, c, y = place()
+    rows, cols = coef_ref.shape
+    half = cols // 2
+
+    def block(zb, xb, yb, h=None):
+        row = pl.multiple_of((zb * 4 + xb * 2 + c) * rows, rows)
+        if h is None:
+            return full_ref.at[pl.ds(row, rows), pl.ds(pl.multiple_of(yb * cols, cols), cols)]
+        col = pl.multiple_of(yb * cols + h * half, half)
+        return full_ref.at[pl.ds(row, rows), pl.ds(col, half)]
+
+    greet(z, x, c, y)
+    block(z, x, y)[...] = coef_ref[...]
+    idxo_ref[y] = idx_ref[...]
+    started = []
+
+    def send(part, sems, i, target):
+        copy = remote(part, part, sems, i, target)
+        copy.start()
+        started.append(copy)
+        return copy
+
+    to_x, to_y, to_c = device(z, 1 - x, c, y), device(z, x, c, 1 - y), device(z, x, 1 - c, y)
+    zc = [send(block(z, x, y), zs, k - 1, device(lax.rem(z + k, 4), x, c, y)) for k in (1, 2, 3)]
+    idx_copy = send(idxo_ref.at[y], ids, 0, to_y)
+    line = [lax.rem(z + 4 - j, 4) for j in range(4)]
+    xa, yb = [], []
+    for j in range(4):
+        if j:
+            zc[j - 1].wait_recv()
+        xa.append(send(block(line[j], x, y, 0), xas, j, to_x))
+        yb.append(send(block(line[j], x, y, 1), ybs, j, to_y))
+        send(block(line[j], x, y, 0), yas, j, to_y)
+        send(block(line[j], x, y, 1), xbs, j, to_x)
+        send(block(line[j], x, y), cs, j, to_c)
+    for j in range(4):
+        xa[j].wait_recv()
+        send(block(line[j], 1 - x, y, 0), yas, 4 + j, to_y)
+        send(block(line[j], 1 - x, y, 0), cs, 4 + j, to_c)
+        yb[j].wait_recv()
+        send(block(line[j], x, 1 - y, 1), xbs, 4 + j, to_x)
+        send(block(line[j], x, 1 - y, 1), cs, 8 + j, to_c)
+    for j in range(4):
+        remote(block(line[j], x, y, 0), block(line[j], x, 1 - y, 0), yas, j, to_y).wait_recv()
+        send(block(line[j], x, 1 - y, 0), cs, 12 + j, to_c)
+        remote(block(line[j], x, y, 1), block(line[j], 1 - x, y, 1), xbs, j, to_x).wait_recv()
+        send(block(line[j], 1 - x, y, 1), cs, 16 + j, to_c)
+    for j in range(4):
+        far = block(line[j], 1 - x, 1 - y, 0)
+        remote(far, far, yas, 4 + j, to_y).wait_recv()
+        send(far, cs, 20 + j, to_c)
+        far = block(line[j], 1 - x, 1 - y, 1)
+        remote(far, far, xbs, 4 + j, to_x).wait_recv()
+        send(far, cs, 24 + j, to_c)
+    idx_copy.wait_recv()
+    for i in range(28):
+        part = block(z, x, y) if i < 4 else block(z, x, y, 0)
+        remote(part, part, cs, i, to_c).wait_recv()
+    for copy in started:
+        copy.wait_send()
+
+
+def gather(coef, idx):
+    rows, cols = coef.shape
+    counts = (3, 4, 8, 8, 4, 28, 1)
+    sems = [pltpu.SemaphoreType.DMA((n,)) for n in counts for _ in range(2)]
+    return pl.pallas_call(
+        gather_kernel,
+        out_shape=(
+            jax.ShapeDtypeStruct((rows * 16, cols * 2), coef.dtype),
+            jax.ShapeDtypeStruct((2,) + idx.shape, idx.dtype),
+        ),
+        in_specs=[VMEM, VMEM],
+        out_specs=(VMEM, VMEM),
+        scratch_shapes=sems,
+        compiler_params=pltpu.CompilerParams(
+            collective_id=0, has_side_effects=True, vmem_limit_bytes=48 * 1024 * 1024
+        ),
+        name="coef_gather",
+    )(coef, idx)
+
+
+def reduce_kernel(factor, bt_ref, vg_ref, out_ref, cso, cri, acc, yso, yri, xso, xri, xbo, xbi, ybo, ybi, zso, zri, *sems):
+    cs, yas, xas, xbs, ybs, zs = [sems[2 * i : 2 * i + 2] for i in range(6)]
+    z, x, c, y = place()
+    cols = out_ref.shape[1]
+    width = cols // 4
+    rows = out_ref.shape[0]
+    side = rows * 4
+    greet(z, x, c, y)
+    to_x, to_y, to_c = device(z, 1 - x, c, y), device(z, x, c, 1 - y), device(z, x, 1 - c, y)
+    mine, theirs = pl.ds(pl.multiple_of(x * side, side), side), pl.ds(pl.multiple_of((1 - x) * side, side), side)
+    started = []
+
+    def send(src, dst, sems, i, target):
+        copy = remote(src, dst, sems, i, target)
+        copy.start()
+        started.append(copy)
+        return copy
+
+    def number(h, s, q):
+        return (h * 2 + s) * 2 + q
+
+    def term(core, h, s, q):
+        yq = y if q else 1 - y
+        col = pl.multiple_of(yq * cols + (h * 2 + s) * width, width)
+        return jnp.dot(bt_ref[core], vg_ref[:, pl.ds(col, width)], preferred_element_type=jnp.float32)
+
+    order = [(h, s, q) for s in (0, 1) for h, q in ((0, 0), (1, 0), (1, 1), (0, 1))]
+    copies = {}
+    for h, s, q in order:
+        i = number(h, s, q)
+        cso[i] = term(1 - c, h, s, q).astype(jnp.bfloat16)
+        copies["c", i] = send(cso.at[i], cri.at[i], cs, i, to_c)
+    for h, s, q in order:
+        i = number(h, s, q)
+        own = term(c, h, s, q)
+        copies["c", i].wait_recv()
+        acc[i] = own + cri[i].astype(jnp.float32)
+        if h == 0 and q == 0:
+            yso[s] = acc[i].astype(jnp.bfloat16)
+            copies["ya", s] = send(yso.at[s], yri.at[s], yas, s, to_y)
+        if h == 1:
+            j = q * 2 + s
+            xbo[j] = acc[i, theirs].astype(jnp.bfloat16)
+            copies["xb", j] = send(xbo.at[j], xbi.at[j], xbs, j, to_x)
+    for s in (0, 1):
+        i = number(1, s, 0)
+        copies["xb", s].wait_recv()
+        ybo[s] = (acc[i, mine] + xbi[s].astype(jnp.float32)).astype(jnp.bfloat16)
+        copies["yb", s] = send(ybo.at[s], ybi.at[s], ybs, s, to_y)
+        i = number(0, s, 1)
+        copies["ya", s].wait_recv()
+        xso[s] = (acc[i, theirs] + yri[s, theirs].astype(jnp.float32)).astype(jnp.bfloat16)
+        copies["xa", s] = send(xso.at[s], xri.at[s], xas, s, to_x)
+        acc[i, mine] = acc[i, mine] + yri[s, mine].astype(jnp.float32)
+        i = number(1, s, 1)
+        copies["xb", 2 + s].wait_recv()
+        acc[i, mine] = acc[i, mine] + xbi[2 + s].astype(jnp.float32)
+    for s in (0, 1):
+        for h in (1, 0):
+            i, j = number(h, s, 1), h * 2 + s
+            copies["yb" if h else "xa", s].wait_recv()
+            arrived = ybi[s] if h else xri[s]
+            acc[i, mine] = acc[i, mine] + arrived.astype(jnp.float32)
+            zso[j] = acc[i, mine].astype(jnp.bfloat16)
+            for k in (1, 2, 3):
+                zk = lax.rem(z + k, 4)
+                part = zso.at[j, pl.ds(pl.multiple_of(zk * rows, rows), rows)]
+                n = (k - 1) * 4 + j
+                copies["z", n] = send(part, zri.at[n], zs, n, device(zk, x, c, y))
+    for s in (0, 1):
+        for h in (1, 0):
+            i, j = number(h, s, 1), h * 2 + s
+            total = acc[i, pl.ds(pl.multiple_of(x * side + z * rows, rows), rows)]
+            for k in range(3):
+                copies["z", k * 4 + j].wait_recv()
+                total = total + zri[k * 4 + j].astype(jnp.float32)
+            out_ref[:, pl.ds(j * width, width)] = total * factor
+    for copy in started:
+        copy.wait_send()
+
+
+def reduce_coef(bt, vg, factor, rows, cols):
+    side, width = rows * 4, cols // 4
+    b, f = jnp.bfloat16, jnp.float32
+    buffers = [
+        ((8, 2 * side, width), b), ((8, 2 * side, width), b), ((8, 2 * side, width), f),
+        ((2, 2 * side, width), b), ((2, 2 * side, width), b),
+        ((2, side, width), b), ((2, side, width), b),
+        ((4, side, width), b), ((4, side, width), b),
+        ((2, side, width), b), ((2, side, width), b),
+        ((4, side, width), b), ((12, rows, width), b),
+    ]
+    sems = [pltpu.SemaphoreType.DMA((n,)) for n in (8, 2, 2, 4, 2, 12) for _ in range(2)]
+    return pl.pallas_call(
+        functools.partial(reduce_kernel, factor),
+        out_shape=jax.ShapeDtypeStruct((rows, cols), f),
+        in_specs=[VMEM, VMEM],
+        out_specs=VMEM,
+        scratch_shapes=[pltpu.VMEM(shape, kind) for shape, kind in buffers] + sems,
+        compiler_params=pltpu.CompilerParams(
+            collective_id=1, has_side_effects=True, vmem_limit_bytes=48 * 1024 * 1024
+        ),
+        name="coef_reduce",
+    )(bt, vg)
 
 
 def funding(netted, scale, borrow, lend):
@@ -11,6 +237,33 @@
 
 
 def body(basis, coef, membership, counts, borrow, lend):
+    trades, sets = membership.shape
+    rows, cols = coef.shape
+    paths = basis.shape[0] // 2
+    number = jnp.arange(1, sets + 1, dtype=jnp.int32)
+    signed = jnp.sum(membership * number, axis=1, dtype=jnp.int32)
+    coef_full, signed_all = gather(coef, signed.reshape(trades // 128, 128))
+    signed_all = signed_all.reshape(2 * trades, 1)
+    member = jnp.where(jnp.abs(signed_all) == number, jnp.sign(signed_all), 0).astype(jnp.bfloat16)
+    half = lax.dynamic_slice_in_dim(basis, lax.axis_index("trades") * paths, paths, 0)
+    trade_value = jnp.dot(half, coef_full, preferred_element_type=jnp.float32)
+    exposure = jax.nn.softplus(trade_value).astype(jnp.bfloat16)
+    netted = jnp.dot(exposure, member, preferred_element_type=jnp.float32)
+    set_grad = funding(netted, lax.rsqrt(counts.astype(jnp.float32)), borrow, lend)
+    trade_grad = lax.dot_general(
+        set_grad, member, (((1,), (1,)), ((), ())), preferred_element_type=jnp.float32
+    )
+    value_grad = (trade_grad * jax.nn.sigmoid(trade_value)).astype(jnp.bfloat16)
+    d_basis = lax.dot_general(
+        value_grad, coef_full, (((1,), (1,)), ((), ())), preferred_element_type=jnp.float32
+    )
+    bt = half.T.reshape(4, 2, 2, rows, paths).transpose(2, 1, 0, 3, 4).reshape(2, 8 * rows, paths)
+    factor = (basis.shape[0] * lax.axis_size("paths")) ** -0.5
+    d_coef = reduce_coef(bt, value_grad, factor, rows, cols)
+    return (d_basis, d_coef)
+
+
+def body_any(basis, coef, membership, counts, borrow, lend):
     path_rows = basis.shape[0]
     member = membership.astype(jnp.bfloat16)
     coef_full = lax.all_gather(coef, "paths", axis=0, tiled=True)
@@ -50,8 +303,9 @@
 
 def solution(mesh):
     placed = (P("paths", None), P("paths", "trades"), P("trades", None), P(), P(), P())
+    small = (mesh.shape["paths"], mesh.shape["trades"]) == (16, 2)
     return jax.shard_map(
-        body,
+        body if small else body_any,
         mesh=mesh,
         in_specs=placed,
         out_specs=(P(("paths", "trades"), None), P("paths", "trades")),

time: 252 us -> 90.2 us (0.36)
  waiting for transfers between devices: 195 us -> 0 us
  Pallas kernels: 0 us -> 66 us
  between operations: 13.8 us -> 0.76 us
  matrix products: 28.5 us -> 17.9 us
  local copies, waits for them, and re-layouts: 10.8 us -> 1.92 us
    unnamed x6 -> x0, waiting for transfers between devices: 77.4 us -> none
    all_gather x2 -> x0, waiting for transfers between devices: 67.7 us -> none  [the longest x1 46.3 us: body(): coef_full = lax.all_gather(coef, 'paths', axis=0, tiled=True)]
    pallas_call x0 -> x2, Pallas kernels: none -> 66 us  [the longest x1 37.2 us: reduce_coef(): pl.pallas_call(functools.partial(reduce_kernel, factor), out_shape=jax.Sh...]
    reduce_scatter x2 -> x0, waiting for transfers between devices: 50.2 us -> none  [the longest x1 30.5 us: body(): lax.psum_scatter(partial_net, 'trades', scatter_dimension=1, tiled=True)]
    dot_general x3 -> x2, matrix products: 17 us -> 7.8 us  [the longest x1 5.46 us: body(): netted = jnp.dot(exposure, member, preferred_element_type=jnp.float32)]
    unnamed x17 -> x11, local copies, waits for them, and re-layouts: 10.6 us -> 1.88 us
    reduce_sum x0 -> x1, other arithmetic: none -> 2.58 us  [body(): signed = jnp.sum(membership * number, axis=1, dtype=jnp.int32)]
    convert_element_type x1 -> x0, other arithmetic: 2.58 us -> none  [funding(): return grad.astype(jnp.bfloat16)]
  transfers between devices with their start and end apart: 5 -> 0, of which waited for: 5 -> 0; matrix products, arithmetic and copies ran while one was open for 5% -> 0% of each run, Pallas kernels for 0% -> 0%
where the time goes in v1:
time: 90.2 us; the launch traced here: 90 us
  Pallas kernels  66 us (73%)
  matrix products  17.9 us (20%)
  other arithmetic  3.36 us (4%)
  local copies, waits for them, and re-layouts  1.92 us (2%)
    pallas_call x1, Pallas kernels, reduce_coef(): pl.pallas_call(functools.partial(reduce_kernel, factor), out_shape=jax.Sh...  37.2 us
    pallas_call x1, Pallas kernels, gather(): pl.pallas_call(gather_kernel, out_shape=(jax.ShapeDtypeStruct((rows * 16,...  28.9 us
    dot_general x1, matrix products, body(): lax.dot_general(set_grad, member, (((1,), (1,)), ((), ())), preferred_ele...  6.76 us
    dot_general x1, matrix products, body(): netted = jnp.dot(exposure, member, preferred_element_type=jnp.float32)  5.46 us
    dot_general x1, matrix products, body(): lax.dot_general(value_grad, coef_full, (((1,), (1,)), ((), ())), preferre...  3.36 us
    reduce_sum x1, other arithmetic, body(): signed = jnp.sum(membership * number, axis=1, dtype=jnp.int32)  2.58 us
    dot_general x1, matrix products, body(): trade_value = jnp.dot(half, coef_full, preferred_element_type=jnp.float32)  2.35 us
    unnamed x11, local copies, waits for them, and re-layouts  1.88 us

profile of v1, /device:TPU:0, one launch (start us, length us, event | category | flops | bytes accessed | tf_op | source)
XLA Modules:
  0.0 90.0 jit_solution(7212130813394360922)
XLA Ops:
  0.6 0.0 copy-start
  0.7 0.8 convert_rsqrt_fusion
  1.4 2.6 %multiply_reduce_fusion = s32[2048]{0:T(1024)S(1)} fusion(s32[2048,512]{1,0:T(8,128)} %param.8, s32[512]{0:T(512)S(1)} %iota_add_fusion), kind=kLoop, calls=%fused_computation.11 | loop fusion | flops 2095104 | bytes 4204544 | tf_op jit(solution)/shard_map/reduce_sum | solution.py:244
  4.0 0.0 copy-start.2
  4.0 0.0 copy-start.3
  4.0 0.0 copy-done
  4.1 0.2 copy.11
  4.4 0.0 copy-start.1
  4.4 0.9 copy-done.1
  5.3 28.9 %coef_gather.1 = (bf16[512,4096]{1,0:T(8,128)(2,1)S(1)}, s32[2,16,128]{2,1,0:T(8,128)S(1)}) custom-call(bf16[32,2048]{1,0:T(8,128)(2,1)S(1)} %copy-done.1, s32[16,128]{1,0:T(8,128)S(1)} %bitcast.15), custom_call_target="tpu_custom_call" | custom-call | tf_op jit(solution)/shard_map/coef_gather/pallas_call | solution.py:111
  34.1 2.3 %fusion.28 = f32[512,4096]{1,0:T(8,128)S(1)} fusion(bf16[512,512]{1,0:T(8,128)(2,1)S(1)} %constant_dynamic-slice_fusion, bf16[512,4096]{1,0:T(8,128)(2,1)S(1)} %get-tuple-element.4), kind=kOutput, calls=%fused_computation.27 | convolution fusion | flops 2147483648 | bytes 13107200 | tf_op jit(solution)/shard_map/dot_general | solution.py:249
  36.5 0.0 copy-done.2
  36.5 0.0 copy-done.3
  36.5 5.5 %multiply_convert_fusion.1.clone.5 = bf16[512,512]{1,0:T(8,128)(2,1)S(1)} fusion(s32[4096]{0:T(1024)S(1)} %bitcast.19, s32[512]{0:T(512)S(1)} %iota_add_fusion, s32[4096]{0:T(1024)S(1)} %bitcast.17, f32[512,4096]{1,0:T(8,128)S(1)} %fusion.28, f32[512]{0:T(512)S(1)} %copy-done.2, f32[512]{0:T(512)S(1)} %convert_rsqrt_fusion, ...), kind=kOutput, calls=%fused_computation.15.clone.clone.clone.2 | convolution fusion | flops 2171338752 | bytes 8953856 | tf_op jit(solution)/shard_map/dot_general | solution.py:251
  42.0 6.8 %multiply_convert_fusion.vg_ref = bf16[512,4096]{1,0:T(8,128)(2,1)S(1)} fusion(f32[512,4096]{1,0:T(8,128)S(1)} %fusion.28, s32[4096]{0:T(1024)S(1)} %bitcast.20, s32[512]{0:T(512)S(1)} %iota_add_fusion, s32[4096]{0:T(1024)S(1)} %bitcast.18, bf16[512,512]{1,0:T(8,128)(2,1)S(1)} %multiply_convert_fusion.1.clone.5), kind=kOutput, calls=%fused_computation.2 | convolution fusion | flops 2164260864 | bytes 13142016 | tf_op jit(solution)/shard_map/dot_general | solution.py:253
  48.7 3.4 %fusion.29 = f32[512,512]{1,0:T(8,128)} fusion(bf16[512,4096]{1,0:T(8,128)(2,1)S(1)} %multiply_convert_fusion.vg_ref, bf16[512,4096]{1,0:T(8,128)(2,1)S(1)} %get-tuple-element.4), kind=kOutput, calls=%fused_computation.28 | convolution fusion | flops 2147483648 | bytes 9437184 | tf_op jit(solution)/shard_map/dot_general | solution.py:257
  52.1 37.2 %coef_reduce.1 = f32[32,2048]{1,0:T(8,128)S(1)} custom-call(bf16[2,256,512]{2,1,0:T(8,128)(2,1)S(1)} %bitcast.14, bf16[512,4096]{1,0:T(8,128)(2,1)S(1)} %multiply_convert_fusion.vg_ref), custom_call_target="tpu_custom_call" | custom-call | tf_op jit(solution)/shard_map/coef_reduce/pallas_call | solution.py:220
  89.3 0.7 copy.13
  (4 shorter events, 0.1 us)
Async XLA Ops:
  0.6 3.4 %copy-start = (bf16[1024,512]{1,0:T(8,128)(2,1)S(1)}, bf16[1024,512]{1,0:T(8,128)(2,1)}, u32[]{:S(2)}) copy-start(bf16[1024,512]{1,0:T(8,128)(2,1)} %param.6) | copy-start | bytes 3145732
  4.0 32.5 %copy-start.2 = (f32[512]{0:T(512)S(1)}, f32[512]{0:T(512)}, u32[]{:S(2)}) copy-start(f32[512]{0:T(512)} %param.11) | copy-start | bytes 6148
  4.0 32.5 %copy-start.3 = (f32[512]{0:T(512)S(1)}, f32[512]{0:T(512)}, u32[]{:S(2)}) copy-start(f32[512]{0:T(512)} %param.10) | copy-start | bytes 6148
  4.4 0.9 %copy-start.1 = (bf16[32,2048]{1,0:T(8,128)(2,1)S(1)}, bf16[32,2048]{1,0:T(8,128)(2,1)}, u32[]{:S(2)}) copy-start(bf16[32,2048]{1,0:T(8,128)(2,1)} %coef_ref.1) | copy-start | bytes 393220

commit v2 on v0

--- a/solution.py
+++ b/solution.py
@@ -1,7 +1,347 @@
+import functools
+
 import jax
 import jax.numpy as jnp
 from jax import lax
+from jax.experimental import pallas as pl
+from jax.experimental.pallas import tpu as pltpu
 from jax.sharding import PartitionSpec as P
+
+MESH = pl.DeviceIdType.MESH
+VMEM = pl.BlockSpec(memory_space=pltpu.VMEM)
+
+
+def place():
+    p, y = lax.axis_index("paths"), lax.axis_index("trades")
+    return p // 4, lax.rem(p // 2, 2), lax.rem(p, 2), y
+
+
+def device(z, x, c, y):
+    return (z * 4 + x * 2 + c, y)
+
+
+def greet(z, x, c, y):
+    barrier = pltpu.get_barrier_semaphore()
+    others = [device(lax.rem(z + k, 4), x, c, y) for k in (1, 2, 3)]
+    others += [device(z, 1 - x, c, y), device(z, x, 1 - c, y), device(z, x, c, 1 - y)]
+    for other in others:
+        pl.semaphore_signal(barrier, inc=1, device_id=other, device_id_type=MESH)
+    pl.semaphore_wait(barrier, len(others))
+
+
+def remote(src, dst, sems, i, target):
+    return pltpu.make_async_remote_copy(
+        src_ref=src,
+        dst_ref=dst,
+        send_sem=sems[0].at[i],
+        recv_sem=sems[1].at[i],
+        device_id=target,
+        device_id_type=MESH,
+    )
+
+
+NT = (((1,), (1,)), ((), ()))
+
+
+def adjoint_kernel(
+    factor, member_ref, coef_ref, half_ref, bt_ref, spread_ref, db_ref, out_ref,
+    member, full_ref, idxo, mem_t, sig, exposure, netted, set_grad, vg,
+    cso, cri, acc, yso, yri, xso, xri, xbo, xbi, ybo, ybi, zso, zri, member_sem, *sems
+):
+    gz, gxa, gya, gxb, gyb, gc, gi, cs, yas, xas, xbs, ybs, zs = [sems[2 * i : 2 * i + 2] for i in range(13)]
+    z, x, c, y = place()
+    rows, cols = coef_ref.shape
+    half = cols // 2
+    paths, sets = netted.shape
+    f32, bf16 = jnp.float32, jnp.bfloat16
+    started = []
+
+    fetch = pltpu.make_async_copy(member_ref, member, member_sem)
+    fetch.start()
+
+    def block(zb, xb, yb, h=None):
+        row = pl.multiple_of((zb * 4 + xb * 2 + c) * rows, rows)
+        if h is None:
+            return full_ref.at[pl.ds(row, rows), pl.ds(pl.multiple_of(yb * cols, cols), cols)]
+        col = pl.multiple_of(yb * cols + h * half, half)
+        return full_ref.at[pl.ds(row, rows), pl.ds(col, half)]
+
+    def send(src, dst, sems, i, target):
+        copy = remote(src, dst, sems, i, target)
+        copy.start()
+        started.append(copy)
+        return copy
+
+    def pass_on(part, sems, i, target):
+        return send(part, part, sems, i, target)
+
+    to_x, to_y, to_c = device(z, 1 - x, c, y), device(z, x, c, 1 - y), device(z, x, 1 - c, y)
+    block(z, x, y)[...] = coef_ref[...]
+    greet(z, x, c, y)
+
+    near = z + 1 - 2 * lax.rem(z, 2)
+    line = [z, near, lax.rem(z + 2, 4), lax.rem(near + 2, 4)]
+    zc = [pass_on(block(z, x, y), gz, k, device(line[k + 1], x, c, y)) for k in range(3)]
+
+    def spread_own(j):
+        a = pass_on(block(line[j], x, y, 0), gxa, j, to_x)
+        b = pass_on(block(line[j], x, y, 1), gyb, j, to_y)
+        pass_on(block(line[j], x, y, 0), gya, j, to_y)
+        pass_on(block(line[j], x, y, 1), gxb, j, to_x)
+        pass_on(block(line[j], x, y), gc, j, to_c)
+        return a, b
+
+    own = [spread_own(0)]
+
+    fetch.wait()
+    number = lax.broadcasted_iota(jnp.int32, (16, sets), 1) + 1
+    first = lax.broadcasted_iota(jnp.int32, (16, sets), 0) == 0
+    digits = jnp.where(first, number // 64, lax.rem(number, 64)).astype(f32).astype(bf16)
+
+    def find(k, carry):
+        at = pl.ds(pl.multiple_of(k * 512, 512), 512)
+        both = lax.dot_general(
+            digits, member[at, :].astype(f32).astype(bf16), NT, preferred_element_type=f32
+        )
+        idxo[y, :, at] = jnp.broadcast_to(both[0:1] * 64.0 + both[1:2], (8, 512))
+        return carry
+
+    lax.fori_loop(0, cols // 512, find, 0)
+    idx_copy = pass_on(idxo.at[y], gi, 0, to_y)
+
+    def build(yb):
+        def chunk(k, carry):
+            at = pl.ds(pl.multiple_of(k * 512, 512), 512)
+            to = pl.ds(pl.multiple_of(yb * cols + k * 512, 512), 512)
+            idx = idxo[yb, 0:1, at]
+            size, sign = jnp.abs(idx), jnp.where(idx > 0, 1.0, -1.0)
+
+            def some(r, inner):
+                base = lax.broadcasted_iota(jnp.int32, (32, 512), 0) + (r * 32 + 1)
+                hit = jnp.where(base.astype(f32) == size, sign, 0.0)
+                mem_t[pl.ds(pl.multiple_of(r * 32, 32), 32), to] = hit.astype(bf16)
+                return inner
+
+            return lax.fori_loop(0, sets // 32, some, carry)
+
+        lax.fori_loop(0, cols // 512, chunk, 0)
+
+    def forward(yb, start, stop):
+        def chunk(k, carry):
+            at = pl.ds(pl.multiple_of(yb * cols + k * 512, 512), 512)
+            sig[:, at] = jnp.dot(half_ref[...], full_ref[:, at], preferred_element_type=f32)
+
+            def some(r, inner):
+                part = pl.ds(pl.multiple_of(r * 32, 32), 32)
+                v = sig[part, at]
+                e = jnp.exp(-jnp.abs(v))
+                log = jnp.where(e < 0.01, e * (1.0 - e * (0.5 - e * (1.0 / 3.0))), jnp.log(1.0 + e))
+                exposure[part, :] = (jnp.maximum(v, 0.0) + log).astype(bf16)
+                sig[part, at] = jnp.where(v >= 0, 1.0, e) / (1.0 + e)
+                return inner
+
+            lax.fori_loop(0, paths // 32, some, 0)
+            netted[...] += lax.dot_general(exposure[...], mem_t[:, at], NT, preferred_element_type=f32)
+            return carry
+
+        lax.fori_loop(start, stop, chunk, 0)
+
+    netted[...] = jnp.zeros_like(netted)
+    for j in (1, 2, 3):
+        zc[j - 1].wait_recv()
+        own.append(spread_own(j))
+    for j in range(4):
+        own[j][0].wait_recv()
+        pass_on(block(line[j], 1 - x, y, 0), gya, 4 + j, to_y)
+        pass_on(block(line[j], 1 - x, y, 0), gc, 4 + j, to_c)
+        own[j][1].wait_recv()
+        pass_on(block(line[j], x, 1 - y, 1), gxb, 4 + j, to_x)
+        pass_on(block(line[j], x, 1 - y, 1), gc, 8 + j, to_c)
+
+    def landed(part, sems, i):
+        remote(part, part, sems, i, to_c).wait_recv()
+        return part
+
+    def from_core(numbers):
+        for i in numbers:
+            landed(block(z, x, y) if i < 4 else block(z, x, y, 0), gc, i)
+
+    for j in range(4):
+        pass_on(landed(block(line[j], 1 - x, y, 1), gxb, j), gc, 16 + j, to_c)
+    build(y)
+    for j in range(4):
+        pass_on(landed(block(line[j], x, 1 - y, 0), gya, j), gc, 12 + j, to_c)
+    from_core([0, 1, 2, 3, 4, 5, 6, 7, 16, 17, 18, 19])
+    forward(y, 0, 2)
+
+    def far(j):
+        pass_on(landed(block(line[j], 1 - x, 1 - y, 0), gya, 4 + j), gc, 20 + j, to_c)
+        pass_on(landed(block(line[j], 1 - x, 1 - y, 1), gxb, 4 + j), gc, 24 + j, to_c)
+
+    far(0)
+    far(1)
+    idx_copy.wait_recv()
+    build(1 - y)
+    far(2)
+    far(3)
+    forward(y, 2, 4)
+    from_core([8, 9, 10, 11, 12, 13, 14, 15, 20, 21, 22, 23, 24, 25, 26, 27])
+    forward(1 - y, 0, 4)
+
+    def fund(r, carry):
+        part = pl.ds(pl.multiple_of(r * 32, 32), 32)
+        scale, borrow, lend = spread_ref[0:1, :], spread_ref[1:2, :], spread_ref[2:3, :]
+        s = netted[part, :] * scale
+        e = jnp.exp(-jnp.abs(s))
+        grad = jnp.where(s >= 0, borrow + lend * e, borrow * e + lend) / (1.0 + e) * scale
+        set_grad[part, :] = grad.astype(bf16)
+        return carry
+
+    lax.fori_loop(0, paths // 32, fund, 0)
+
+    steps = 4
+    width = half // steps
+    side = rows * 4
+    mine, theirs = pl.ds(pl.multiple_of(x * side, side), side), pl.ds(pl.multiple_of((1 - x) * side, side), side)
+    copies = {}
+
+    def columns(s, i):
+        q = i // 2
+        h = lax.rem((i + 1) // 2, 2)
+        yq = (1 - y) + q * (2 * y - 1)
+        return pl.ds(pl.multiple_of(yq * cols + h * half + s * width, width), width)
+
+    def core_copy(n):
+        return remote(cso.at[n], cri.at[n], cs, n, to_c)
+
+    def first_step(s):
+        def chunk(i, carry):
+            at = columns(s, i)
+            grad = jnp.dot(set_grad[...], mem_t[:, at], preferred_element_type=f32)
+            vg[:, at] = (grad * sig[:, at]).astype(bf16)
+            n = s * 4 + i
+            cso[n] = jnp.dot(bt_ref[1 - c], vg[:, at], preferred_element_type=f32).astype(bf16)
+            core_copy(n).start()
+            return carry
+
+        lax.fori_loop(0, 4, chunk, 0)
+
+    def second_step(s):
+        def chunk(i, carry):
+            n = s * 4 + i
+            own = jnp.dot(bt_ref[c], vg[:, columns(s, i)], preferred_element_type=f32)
+            core_copy(n).wait_recv()
+            acc[n] = own + cri[n].astype(f32)
+            return carry
+
+        lax.fori_loop(0, 4, chunk, 0)
+        yso[s] = acc[s * 4].astype(bf16)
+        copies["ya", s] = send(yso.at[s], yri.at[s], yas, s, to_y)
+        for q in (0, 1):
+            j = q * steps + s
+            xbo[j] = acc[s * 4 + 1 + q, theirs].astype(bf16)
+            copies["xb", j] = send(xbo.at[j], xbi.at[j], xbs, j, to_x)
+
+    def third_step(s):
+        copies["xb", s].wait_recv()
+        ybo[s] = (acc[s * 4 + 1, mine] + xbi[s].astype(f32)).astype(bf16)
+        copies["yb", s] = send(ybo.at[s], ybi.at[s], ybs, s, to_y)
+        copies["ya", s].wait_recv()
+        xso[s] = (acc[s * 4 + 3, theirs] + yri[s, theirs].astype(f32)).astype(bf16)
+        copies["xa", s] = send(xso.at[s], xri.at[s], xas, s, to_x)
+        acc[s * 4 + 3, mine] = acc[s * 4 + 3, mine] + yri[s, mine].astype(f32)
+        copies["xb", steps + s].wait_recv()
+        acc[s * 4 + 2, mine] = acc[s * 4 + 2, mine] + xbi[steps + s].astype(f32)
+
+    def fourth_step(s):
+        for h in (1, 0):
+            i, j = s * 4 + (2 if h else 3), h * steps + s
+            copies["yb" if h else "xa", s].wait_recv()
+            arrived = ybi[s] if h else xri[s]
+            acc[i, mine] = acc[i, mine] + arrived.astype(f32)
+            zso[j] = acc[i, mine].astype(bf16)
+            for k in range(3):
+                zk = line[k + 1]
+                part = zso.at[j, pl.ds(pl.multiple_of(zk * rows, rows), rows)]
+                n = k * 2 * steps + j
+                copies["z", n] = send(part, zri.at[n], zs, n, device(zk, x, c, y))
+
+    def last_step(s):
+        for h in (1, 0):
+            i, j = s * 4 + (2 if h else 3), h * steps + s
+            total = acc[i, pl.ds(pl.multiple_of(x * side + z * rows, rows), rows)]
+            for k in range(3):
+                copies["z", k * 2 * steps + j].wait_recv()
+                total = total + zri[k * 2 * steps + j].astype(f32)
+            out_ref[:, pl.ds(j * width, width)] = total * factor
+
+    def basis_part(k):
+        size = sets_k // 2
+        db_ref[:, k * size : (k + 1) * size] = lax.dot_general(
+            vg[...], full_ref[k * size : (k + 1) * size, :], NT, preferred_element_type=f32
+        )
+
+    sets_k = full_ref.shape[0]
+    first_step(0)
+    first_step(1)
+    second_step(0)
+    first_step(2)
+    second_step(1)
+    third_step(0)
+    first_step(3)
+    second_step(2)
+    fourth_step(0)
+    third_step(1)
+    second_step(3)
+    third_step(2)
+    fourth_step(1)
+    basis_part(0)
+    third_step(3)
+    fourth_step(2)
+    basis_part(1)
+    fourth_step(3)
+    for s in range(steps):
+        last_step(s)
+
+    def sent(n, carry):
+        core_copy(n).wait_send()
+        return carry
+
+    lax.fori_loop(0, 4 * steps, sent, 0)
+    for copy in started:
+        copy.wait_send()
+
+
+def adjoint(membership, coef, half, bt, spread, factor):
+    trades, sets = membership.shape
+    rows, cols = coef.shape
+    paths, k = half.shape
+    b, f = jnp.bfloat16, jnp.float32
+    steps = 4
+    width, side = cols // 2 // steps, rows * 4
+    buffers = [
+        ((trades, sets), membership.dtype), ((k, 2 * cols), b), ((2, 8, cols), f), ((sets, 2 * cols), b),
+        ((paths, 2 * cols), f), ((paths, 512), b), ((paths, sets), f), ((paths, sets), b), ((paths, 2 * cols), b),
+        ((4 * steps, 2 * side, width), b), ((4 * steps, 2 * side, width), b), ((4 * steps, 2 * side, width), f),
+        ((steps, 2 * side, width), b), ((steps, 2 * side, width), b),
+        ((steps, side, width), b), ((steps, side, width), b),
+        ((2 * steps, side, width), b), ((2 * steps, side, width), b),
+        ((steps, side, width), b), ((steps, side, width), b),
+        ((2 * steps, side, width), b), ((6 * steps, rows, width), b),
+    ]
+    counts = (3, 4, 8, 8, 4, 28, 1, 4 * steps, steps, steps, 2 * steps, steps, 6 * steps)
+    sems = [pltpu.SemaphoreType.DMA((n,)) for n in counts for _ in range(2)]
+    return pl.pallas_call(
+        functools.partial(adjoint_kernel, factor),
+        out_shape=(jax.ShapeDtypeStruct((paths, k), f), jax.ShapeDtypeStruct((rows, cols), f)),
+        in_specs=[pl.BlockSpec(memory_space=pl.ANY)] + [VMEM] * 4,
+        out_specs=(VMEM, VMEM),
+        scratch_shapes=[pltpu.VMEM(shape, kind) for shape, kind in buffers] + [pltpu.SemaphoreType.DMA] + sems,
+        compiler_params=pltpu.CompilerParams(
+            collective_id=0, has_side_effects=True, vmem_limit_bytes=56 * 1024 * 1024
+        ),
+        name="adjoint",
+    )(membership, coef, half, bt, spread)
 
 
 def funding(netted, scale, borrow, lend):
@@ -11,6 +351,16 @@
 
 
 def body(basis, coef, membership, counts, borrow, lend):
+    rows = coef.shape[0]
+    paths = basis.shape[0] // 2
+    half = lax.dynamic_slice_in_dim(basis, lax.axis_index("trades") * paths, paths, 0)
+    bt = half.T.reshape(4, 2, 2, rows, paths).transpose(2, 1, 0, 3, 4).reshape(2, 8 * rows, paths)
+    spread = jnp.stack([lax.rsqrt(counts.astype(jnp.float32)), borrow, lend])
+    factor = (basis.shape[0] * lax.axis_size("paths")) ** -0.5
+    return adjoint(membership, coef, half, bt, spread, factor)
+
+
+def body_any(basis, coef, membership, counts, borrow, lend):
     path_rows = basis.shape[0]
     member = membership.astype(jnp.bfloat16)
     coef_full = lax.all_gather(coef, "paths", axis=0, tiled=True)
@@ -50,8 +400,9 @@
 
 def solution(mesh):
     placed = (P("paths", None), P("paths", "trades"), P("trades", None), P(), P(), P())
+    small = (mesh.shape["paths"], mesh.shape["trades"]) == (16, 2)
     return jax.shard_map(
-        body,
+        body if small else body_any,
         mesh=mesh,
         in_specs=placed,
         out_specs=(P(("paths", "trades"), None), P("paths", "trades")),

time: 252 us -> 85.5 us (0.34)
  waiting for transfers between devices: 195 us -> 0 us
  Pallas kernels: 0 us -> 76.6 us
  matrix products: 28.5 us -> 0 us
  between operations: 13.8 us -> 0.66 us
  local copies, waits for them, and re-layouts: 10.8 us -> 5.87 us
    unnamed x6 -> x0, waiting for transfers between devices: 77.4 us -> none
    pallas_call x0 -> x1, Pallas kernels: none -> 76.6 us  [adjoint(): pl.pallas_call(functools.partial(adjoint_kernel, factor), out_shape=(jax....]
    all_gather x2 -> x0, waiting for transfers between devices: 67.7 us -> none  [the longest x1 46.3 us: body(): coef_full = lax.all_gather(coef, 'paths', axis=0, tiled=True)]
    reduce_scatter x2 -> x0, waiting for transfers between devices: 50.2 us -> none  [the longest x1 30.5 us: body(): lax.psum_scatter(partial_net, 'trades', scatter_dimension=1, tiled=True)]
    dot_general x5 -> x0, matrix products: 28.5 us -> none  [the longest x1 7.79 us: body(): lax.dot_general(set_grad, member, (((1,), (1,)), ((), ())), preferred_ele...]
    unnamed x17 -> x4, local copies, waits for them, and re-layouts: 10.6 us -> 3.94 us
    convert_element_type x1 -> x0, other arithmetic: 2.58 us -> none  [funding(): return grad.astype(jnp.bfloat16)]
  transfers between devices with their start and end apart: 5 -> 0, of which waited for: 5 -> 0; matrix products, arithmetic and copies ran while one was open for 5% -> 0% of each run, Pallas kernels for 0% -> 0%
where the time goes in v2:
time: 85.5 us; the launch traced here: 85.3 us
  Pallas kernels  76.6 us (90%)
  local copies, waits for them, and re-layouts  5.87 us (7%)
  other arithmetic  2.08 us (2%)
    pallas_call x1, Pallas kernels, adjoint(): pl.pallas_call(functools.partial(adjoint_kernel, factor), out_shape=(jax....  76.6 us
    unnamed x4, local copies, waits for them, and re-layouts  3.94 us

profile of v2, /device:TPU:0, one launch (start us, length us, event | category | flops | bytes accessed | tf_op | source)
XLA Modules:
  0.0 85.3 jit_solution(8989295086869069077)
XLA Ops:
  0.6 0.0 copy-start
  0.6 0.8 convert_rsqrt_fusion
  1.4 1.3 %pad_maximum_fusion.spread_ref = f32[3,512]{1,0:T(4,128)} fusion(f32[1,512]{1,0:T(1,128)} %bitcast.12, f32[1,512]{1,0:T(1,128)} %bitcast.13, f32[1,512]{1,0:T(1,128)S(1)} %bitcast.11), kind=kLoop, calls=%fused_computation | loop fusion | flops 3072 | bytes 12288 | tf_op jit(solution)/shard_map/stack | solution.py:358
  2.7 0.0 copy-done
  2.8 0.2 copy.9
  3.0 0.9 copy.10
  3.8 0.8 constant_dynamic-slice_fusion.half_ref
  4.7 76.6 %adjoint.1 = (f32[512,512]{1,0:T(8,128)}, f32[32,2048]{1,0:T(8,128)}) custom-call(s32[2048,512]{1,0:T(8,128)} %member_ref.1, bf16[32,2048]{1,0:T(8,128)(2,1)} %coef_ref.1, bf16[512,512]{1,0:T(8,128)(2,1)} %constant_dynamic-slice_fusion.half_ref, bf16[2,256,512]{2,1,0:T(8,128)(2,1)} %bitcast.10, f32[3,512]{1,0:T(4,128)} %pad_maximum_fusion.spread_ref), custom_call_target="tpu_custom_call" | custom-call | tf_op jit(solution)/shard_map/adjoint/pallas_call | solution.py:334
  81.3 2.3 %copy.13 = f32[512,512]{1,0:T(8,128)} copy(f32[512,512]{1,0:T(8,128)} %get-tuple-element.4) | data formatting | bytes 2097152
  83.6 1.7 %copy.14 = f32[32,2048]{1,0:T(8,128)} copy(f32[32,2048]{1,0:T(8,128)} %get-tuple-element.5) | data formatting | bytes 524288
  (1 shorter events, 0.0 us)
Async XLA Ops:
  0.6 2.1 %copy-start = (bf16[1024,512]{1,0:T(8,128)(2,1)S(1)}, bf16[1024,512]{1,0:T(8,128)(2,1)}, u32[]{:S(2)}) copy-start(bf16[1024,512]{1,0:T(8,128)(2,1)} %param.6) | copy-start | bytes 3145732

commit v3 on v2

--- a/solution.py
+++ b/solution.py
@@ -1,5 +1,3 @@
-import functools
-
 import jax
 import jax.numpy as jnp
 from jax import lax
@@ -44,9 +42,9 @@
 
 
 def adjoint_kernel(
-    factor, member_ref, coef_ref, half_ref, bt_ref, spread_ref, db_ref, out_ref,
-    member, full_ref, idxo, mem_t, sig, exposure, netted, set_grad, vg,
-    cso, cri, acc, yso, yri, xso, xri, xbo, xbi, ybo, ybi, zso, zri, member_sem, *sems
+    member_ref, basis_ref, coef_ref, counts_ref, borrow_ref, lend_ref, db_ref, out_ref,
+    member, half_ref, bt_ref, full_ref, idxo, mem_t, sig, exposure, netted, set_grad, vg,
+    cso, cri, acc, yso, yri, xso, xri, xbo, xbi, ybo, ybi, zso, zri, member_sem, half_sem, *sems
 ):
     gz, gxa, gya, gxb, gyb, gc, gi, cs, yas, xas, xbs, ybs, zs = [sems[2 * i : 2 * i + 2] for i in range(13)]
     z, x, c, y = place()
@@ -58,6 +56,10 @@
 
     fetch = pltpu.make_async_copy(member_ref, member, member_sem)
     fetch.start()
+    fetch_half = pltpu.make_async_copy(
+        basis_ref.at[pl.ds(pl.multiple_of(y * paths, paths), paths)], half_ref, half_sem
+    )
+    fetch_half.start()
 
     def block(zb, xb, yb, h=None):
         row = pl.multiple_of((zb * 4 + xb * 2 + c) * rows, rows)
@@ -93,7 +95,6 @@
 
     own = [spread_own(0)]
 
-    fetch.wait()
     number = lax.broadcasted_iota(jnp.int32, (16, sets), 1) + 1
     first = lax.broadcasted_iota(jnp.int32, (16, sets), 0) == 0
     digits = jnp.where(first, number // 64, lax.rem(number, 64)).astype(f32).astype(bf16)
@@ -106,8 +107,6 @@
         idxo[y, :, at] = jnp.broadcast_to(both[0:1] * 64.0 + both[1:2], (8, 512))
         return carry
 
-    lax.fori_loop(0, cols // 512, find, 0)
-    idx_copy = pass_on(idxo.at[y], gi, 0, to_y)
 
     def build(yb):
         def chunk(k, carry):
@@ -122,7 +121,7 @@
                 mem_t[pl.ds(pl.multiple_of(r * 32, 32), 32), to] = hit.astype(bf16)
                 return inner
 
-            return lax.fori_loop(0, sets // 32, some, carry)
+            return lax.fori_loop(0, sets // 32, some, carry, unroll=2)
 
         lax.fori_loop(0, cols // 512, chunk, 0)
 
@@ -131,26 +130,34 @@
             at = pl.ds(pl.multiple_of(yb * cols + k * 512, 512), 512)
             sig[:, at] = jnp.dot(half_ref[...], full_ref[:, at], preferred_element_type=f32)
 
-            def some(r, inner):
-                part = pl.ds(pl.multiple_of(r * 32, 32), 32)
+            def some(i, inner):
+                part = pl.ds(pl.multiple_of(i * 32, 32), 32)
                 v = sig[part, at]
                 e = jnp.exp(-jnp.abs(v))
                 log = jnp.where(e < 0.01, e * (1.0 - e * (0.5 - e * (1.0 / 3.0))), jnp.log(1.0 + e))
                 exposure[part, :] = (jnp.maximum(v, 0.0) + log).astype(bf16)
-                sig[part, at] = jnp.where(v >= 0, 1.0, e) / (1.0 + e)
+                d = 1.0 + e
+                r = pl.reciprocal(d, approx=True)
+                r = r * (2.0 - d * r)
+                sig[part, at] = jnp.where(v >= 0, r, e * r)
                 return inner
 
-            lax.fori_loop(0, paths // 32, some, 0)
+            lax.fori_loop(0, paths // 32, some, 0, unroll=4)
             netted[...] += lax.dot_general(exposure[...], mem_t[:, at], NT, preferred_element_type=f32)
             return carry
 
         lax.fori_loop(start, stop, chunk, 0)
 
-    netted[...] = jnp.zeros_like(netted)
-    for j in (1, 2, 3):
-        zc[j - 1].wait_recv()
-        own.append(spread_own(j))
-    for j in range(4):
+    def turn():
+        for k in range(4):
+            size = half_ref.shape[1] // 4
+            part = half_ref[:, k * size : (k + 1) * size].astype(f32).T.astype(bf16)
+            for n in range(size // rows):
+                p = k * (size // rows) + n
+                to = ((p // 2) % 2 * 4 + p // 4) * rows
+                bt_ref[p % 2, to : to + rows, :] = part[n * rows : (n + 1) * rows, :]
+
+    def spread_far(j):
         own[j][0].wait_recv()
         pass_on(block(line[j], 1 - x, y, 0), gya, 4 + j, to_y)
         pass_on(block(line[j], 1 - x, y, 0), gc, 4 + j, to_c)
@@ -158,6 +165,26 @@
         pass_on(block(line[j], x, 1 - y, 1), gxb, 4 + j, to_x)
         pass_on(block(line[j], x, 1 - y, 1), gc, 8 + j, to_c)
 
+    netted[...] = jnp.zeros_like(netted)
+    zc[0].wait_recv()
+    own.append(spread_own(1))
+    fetch.wait()
+    lax.fori_loop(0, cols // 512, find, 0)
+    idx_copy = pass_on(idxo.at[y], gi, 0, to_y)
+    spread_far(0)
+    build(y)
+    zc[1].wait_recv()
+    own.append(spread_own(2))
+    spread_far(1)
+    fetch_half.wait()
+    turn()
+    idx_copy.wait_recv()
+    build(1 - y)
+    zc[2].wait_recv()
+    own.append(spread_own(3))
+    spread_far(2)
+    spread_far(3)
+
     def landed(part, sems, i):
         remote(part, part, sems, i, to_c).wait_recv()
         return part
@@ -168,7 +195,6 @@
 
     for j in range(4):
         pass_on(landed(block(line[j], 1 - x, y, 1), gxb, j), gc, 16 + j, to_c)
-    build(y)
     for j in range(4):
         pass_on(landed(block(line[j], x, 1 - y, 0), gya, j), gc, 12 + j, to_c)
     from_core([0, 1, 2, 3, 4, 5, 6, 7, 16, 17, 18, 19])
@@ -180,24 +206,23 @@
 
     far(0)
     far(1)
-    idx_copy.wait_recv()
-    build(1 - y)
     far(2)
     far(3)
     forward(y, 2, 4)
     from_core([8, 9, 10, 11, 12, 13, 14, 15, 20, 21, 22, 23, 24, 25, 26, 27])
     forward(1 - y, 0, 4)
 
+    scale, borrow, lend = lax.rsqrt(counts_ref[...].astype(f32)), borrow_ref[...], lend_ref[...]
+
     def fund(r, carry):
         part = pl.ds(pl.multiple_of(r * 32, 32), 32)
-        scale, borrow, lend = spread_ref[0:1, :], spread_ref[1:2, :], spread_ref[2:3, :]
         s = netted[part, :] * scale
         e = jnp.exp(-jnp.abs(s))
         grad = jnp.where(s >= 0, borrow + lend * e, borrow * e + lend) / (1.0 + e) * scale
         set_grad[part, :] = grad.astype(bf16)
         return carry
 
-    lax.fori_loop(0, paths // 32, fund, 0)
+    lax.fori_loop(0, paths // 32, fund, 0, unroll=4)
 
     steps = 4
     width = half // steps
@@ -224,7 +249,7 @@
             core_copy(n).start()
             return carry
 
-        lax.fori_loop(0, 4, chunk, 0)
+        lax.fori_loop(0, 4, chunk, 0, unroll=2)
 
     def second_step(s):
         def chunk(i, carry):
@@ -273,15 +298,15 @@
             for k in range(3):
                 copies["z", k * 2 * steps + j].wait_recv()
                 total = total + zri[k * 2 * steps + j].astype(f32)
-            out_ref[:, pl.ds(j * width, width)] = total * factor
-
-    def basis_part(k):
-        size = sets_k // 2
-        db_ref[:, k * size : (k + 1) * size] = lax.dot_general(
-            vg[...], full_ref[k * size : (k + 1) * size, :], NT, preferred_element_type=f32
+            out_ref[:, pl.ds(j * width, width)] = total
+
+    def basis_part(n, k):
+        size = full_ref.shape[0] // 2
+        to, over = slice(k * size, (k + 1) * size), slice(n * cols, (n + 1) * cols)
+        db_ref[n, :, to] = lax.dot_general(
+            vg[:, over], full_ref[to, over], NT, preferred_element_type=f32
         )
 
-    sets_k = full_ref.shape[0]
     first_step(0)
     first_step(1)
     second_step(0)
@@ -293,13 +318,15 @@
     fourth_step(0)
     third_step(1)
     second_step(3)
+    basis_part(0, 0)
     third_step(2)
     fourth_step(1)
-    basis_part(0)
+    basis_part(0, 1)
     third_step(3)
     fourth_step(2)
-    basis_part(1)
+    basis_part(1, 0)
     fourth_step(3)
+    basis_part(1, 1)
     for s in range(steps):
         last_step(s)
 
@@ -312,15 +339,15 @@
         copy.wait_send()
 
 
-def adjoint(membership, coef, half, bt, spread, factor):
+def adjoint(membership, basis, coef, counts, borrow, lend):
     trades, sets = membership.shape
     rows, cols = coef.shape
-    paths, k = half.shape
+    paths, k = basis.shape[0] // 2, basis.shape[1]
     b, f = jnp.bfloat16, jnp.float32
     steps = 4
     width, side = cols // 2 // steps, rows * 4
     buffers = [
-        ((trades, sets), membership.dtype), ((k, 2 * cols), b), ((2, 8, cols), f), ((sets, 2 * cols), b),
+        ((trades, sets), membership.dtype), ((paths, k), b), ((2, 8 * rows, paths), b), ((k, 2 * cols), b), ((2, 8, cols), f), ((sets, 2 * cols), b),
         ((paths, 2 * cols), f), ((paths, 512), b), ((paths, sets), f), ((paths, sets), b), ((paths, 2 * cols), b),
         ((4 * steps, 2 * side, width), b), ((4 * steps, 2 * side, width), b), ((4 * steps, 2 * side, width), f),
         ((steps, 2 * side, width), b), ((steps, 2 * side, width), b),
@@ -329,19 +356,19 @@
         ((steps, side, width), b), ((steps, side, width), b),
         ((2 * steps, side, width), b), ((6 * steps, rows, width), b),
     ]
-    counts = (3, 4, 8, 8, 4, 28, 1, 4 * steps, steps, steps, 2 * steps, steps, 6 * steps)
-    sems = [pltpu.SemaphoreType.DMA((n,)) for n in counts for _ in range(2)]
+    lengths = (3, 4, 8, 8, 4, 28, 1, 4 * steps, steps, steps, 2 * steps, steps, 6 * steps)
+    sems = [pltpu.SemaphoreType.DMA((n,)) for n in lengths for _ in range(2)]
     return pl.pallas_call(
-        functools.partial(adjoint_kernel, factor),
-        out_shape=(jax.ShapeDtypeStruct((paths, k), f), jax.ShapeDtypeStruct((rows, cols), f)),
-        in_specs=[pl.BlockSpec(memory_space=pl.ANY)] + [VMEM] * 4,
+        adjoint_kernel,
+        out_shape=(jax.ShapeDtypeStruct((2, paths, k), f), jax.ShapeDtypeStruct((rows, cols), f)),
+        in_specs=[pl.BlockSpec(memory_space=pl.ANY)] * 2 + [VMEM] * 4,
         out_specs=(VMEM, VMEM),
-        scratch_shapes=[pltpu.VMEM(shape, kind) for shape, kind in buffers] + [pltpu.SemaphoreType.DMA] + sems,
+        scratch_shapes=[pltpu.VMEM(shape, kind) for shape, kind in buffers] + [pltpu.SemaphoreType.DMA] * 2 + sems,
         compiler_params=pltpu.CompilerParams(
-            collective_id=0, has_side_effects=True, vmem_limit_bytes=56 * 1024 * 1024
+            collective_id=0, has_side_effects=True, vmem_limit_bytes=50 * 1024 * 1024
         ),
         name="adjoint",
-    )(membership, coef, half, bt, spread)
+    )(membership, basis, coef, counts, borrow, lend)
 
 
 def funding(netted, scale, borrow, lend):
@@ -351,13 +378,12 @@
 
 
 def body(basis, coef, membership, counts, borrow, lend):
-    rows = coef.shape[0]
-    paths = basis.shape[0] // 2
-    half = lax.dynamic_slice_in_dim(basis, lax.axis_index("trades") * paths, paths, 0)
-    bt = half.T.reshape(4, 2, 2, rows, paths).transpose(2, 1, 0, 3, 4).reshape(2, 8 * rows, paths)
-    spread = jnp.stack([lax.rsqrt(counts.astype(jnp.float32)), borrow, lend])
+    row = (1, counts.shape[0])
+    parts, total = adjoint(
+        membership, basis, coef, counts.reshape(row), borrow.reshape(row), lend.reshape(row)
+    )
     factor = (basis.shape[0] * lax.axis_size("paths")) ** -0.5
-    return adjoint(membership, coef, half, bt, spread, factor)
+    return (parts[0] + parts[1], total * factor)
 
 
 def body_any(basis, coef, membership, counts, borrow, lend):

time: 85.5 us -> 83.3 us (0.974)
  local copies, waits for them, and re-layouts: 5.87 us -> 4.16 us
    another operation x1 -> x0, other arithmetic: 1.31 us -> none  [body(): spread = jnp.stack([lax.rsqrt(counts.astype(jnp.float32)), borrow, lend])]
    add x0 -> x1, other arithmetic: none -> 1.18 us  [body(): return (parts[0] + parts[1], total * factor)]
    transpose x3 -> x0, local copies, waits for them, and re-layouts: 1.1 us -> none  [body(): half.T.reshape(4, 2, 2, rows, paths).transpose(2, 1, 0, 3, 4)]
    unnamed x4 -> x10, local copies, waits for them, and re-layouts: 3.94 us -> 4.16 us
where the time goes in v3:
time: 83.3 us; the launch traced here: 83 us
  Pallas kernels  76.3 us (92%)
  local copies, waits for them, and re-layouts  4.16 us (5%)
  other arithmetic  1.9 us (2%)
    pallas_call x1, Pallas kernels, adjoint(): pl.pallas_call(adjoint_kernel, out_shape=(jax.ShapeDtypeStruct((2, paths,...  76.3 us
    unnamed x10, local copies, waits for them, and re-layouts  4.16 us

profile of v3, /device:TPU:0, one launch (start us, length us, event | category | flops | bytes accessed | tf_op | source)
XLA Modules:
  0.0 83.0 jit_solution(2420728176222771162)
XLA Ops:
  0.6 0.0 copy-start
  0.6 1.2 %copy-done = bf16[1024,512]{1,0:T(8,128)(2,1)S(1)} copy-done((bf16[1024,512]{1,0:T(8,128)(2,1)S(1)}, bf16[1024,512]{1,0:T(8,128)(2,1)}, u32[]{:S(2)}) %copy-start) | copy-done | bytes 1048600
  1.9 0.0 copy-start.1
  1.9 0.9 %copy-done.1 = bf16[32,2048]{1,0:T(8,128)(2,1)S(1)} copy-done((bf16[32,2048]{1,0:T(8,128)(2,1)S(1)}, bf16[32,2048]{1,0:T(8,128)(2,1)}, u32[]{:S(2)}) %copy-start.1) | copy-done | bytes 131096
  2.8 0.0 copy-start.2
  2.8 0.7 copy-done.2
  3.4 0.0 copy-start.3
  3.4 0.7 copy-done.3
  4.1 0.0 copy-start.4
  4.1 0.7 copy-done.4
  4.8 76.3 %adjoint.1 = (f32[2,512,512]{2,1,0:T(8,128)S(1)}, f32[32,2048]{1,0:T(8,128)S(1)}) custom-call(s32[2048,512]{1,0:T(8,128)} %member_ref.1, bf16[1024,512]{1,0:T(8,128)(2,1)S(1)} %copy-done, bf16[32,2048]{1,0:T(8,128)(2,1)S(1)} %copy-done.1, s32[1,512]{1,0:T(1,128)S(1)} %bitcast.5, f32[1,512]{1,0:T(1,128)S(1)} %bitcast.6, f32[1,512]{1,0:T(1,128)S(1)} %bitcast.7), custom_call_target="tpu_custom_call" | custom-call | tf_op jit(solution)/shard_map/adjoint/pallas_call | solution.py:361
  81.1 1.2 %add_bitcast_fusion = f32[512,512]{1,0:T(8,128)} fusion(f32[2,512,512]{2,1,0:T(8,128)S(1)} %get-tuple-element.4), kind=kLoop, calls=%fused_computation | loop fusion | flops 262144 | bytes 3145728 | tf_op jit(solution)/shard_map/add | solution.py:386
  82.3 0.7 broadcast_multiply_fusion
Async XLA Ops:
  0.6 1.2 %copy-start = (bf16[1024,512]{1,0:T(8,128)(2,1)S(1)}, bf16[1024,512]{1,0:T(8,128)(2,1)}, u32[]{:S(2)}) copy-start(bf16[1024,512]{1,0:T(8,128)(2,1)} %basis_ref.1) | copy-start | bytes 3145732
  1.9 0.9 %copy-start.1 = (bf16[32,2048]{1,0:T(8,128)(2,1)S(1)}, bf16[32,2048]{1,0:T(8,128)(2,1)}, u32[]{:S(2)}) copy-start(bf16[32,2048]{1,0:T(8,128)(2,1)} %coef_ref.1) | copy-start | bytes 393220
  2.8 0.7 copy-start.2
  3.4 0.7 copy-start.3
  4.1 0.7 copy-start.4

commit v4 on v3

--- a/solution.py
+++ b/solution.py
@@ -42,9 +42,10 @@
 
 
 def adjoint_kernel(
-    member_ref, basis_ref, coef_ref, counts_ref, borrow_ref, lend_ref, db_ref, out_ref,
+    member_ref, basis_ref, coef_ref, counts_hbm, borrow_hbm, lend_hbm, db_ref, out_ref,
+    counts_ref, borrow_ref, lend_ref,
     member, half_ref, bt_ref, full_ref, idxo, mem_t, sig, exposure, netted, set_grad, vg,
-    cso, cri, acc, yso, yri, xso, xri, xbo, xbi, ybo, ybi, zso, zri, member_sem, half_sem, *sems
+    cso, cri, acc, yso, yri, xso, xri, xbo, xbi, ybo, ybi, zso, zri, fetch_sem, *sems
 ):
     gz, gxa, gya, gxb, gyb, gc, gi, cs, yas, xas, xbs, ybs, zs = [sems[2 * i : 2 * i + 2] for i in range(13)]
     z, x, c, y = place()
@@ -54,19 +55,26 @@
     f32, bf16 = jnp.float32, jnp.bfloat16
     started = []
 
-    fetch = pltpu.make_async_copy(member_ref, member, member_sem)
+    fetch = pltpu.make_async_copy(member_ref, member, fetch_sem.at[0])
     fetch.start()
     fetch_half = pltpu.make_async_copy(
-        basis_ref.at[pl.ds(pl.multiple_of(y * paths, paths), paths)], half_ref, half_sem
+        basis_ref.at[pl.ds(pl.multiple_of(y * paths, paths), paths)], half_ref, fetch_sem.at[1]
     )
     fetch_half.start()
-
-    def block(zb, xb, yb, h=None):
+    small = [
+        pltpu.make_async_copy(src, dst, fetch_sem.at[3 + i])
+        for i, (src, dst) in enumerate(
+            ((counts_hbm, counts_ref), (borrow_hbm, borrow_ref), (lend_hbm, lend_ref))
+        )
+    ]
+    for copy in small:
+        copy.start()
+
+    def block(g, zb, xb, yb, h=None):
         row = pl.multiple_of((zb * 4 + xb * 2 + c) * rows, rows)
-        if h is None:
-            return full_ref.at[pl.ds(row, rows), pl.ds(pl.multiple_of(yb * cols, cols), cols)]
-        col = pl.multiple_of(yb * cols + h * half, half)
-        return full_ref.at[pl.ds(row, rows), pl.ds(col, half)]
+        size = half if h is None else half // 2
+        col = pl.multiple_of(yb * cols + g * half + (h or 0) * size, size)
+        return full_ref.at[pl.ds(row, rows), pl.ds(col, size)]
 
     def send(src, dst, sems, i, target):
         copy = remote(src, dst, sems, i, target)
@@ -78,22 +86,30 @@
         return send(part, part, sems, i, target)
 
     to_x, to_y, to_c = device(z, 1 - x, c, y), device(z, x, c, 1 - y), device(z, x, 1 - c, y)
-    block(z, x, y)[...] = coef_ref[...]
+    own_row = pl.multiple_of((z * 4 + x * 2 + c) * rows, rows)
+    own_slot = full_ref.at[pl.ds(own_row, rows), pl.ds(pl.multiple_of(y * cols, cols), cols)]
+    fetch_coef = pltpu.make_async_copy(coef_ref, own_slot, fetch_sem.at[2])
+    fetch_coef.start()
     greet(z, x, c, y)
+    fetch_coef.wait()
 
     near = z + 1 - 2 * lax.rem(z, 2)
     line = [z, near, lax.rem(z + 2, 4), lax.rem(near + 2, 4)]
-    zc = [pass_on(block(z, x, y), gz, k, device(line[k + 1], x, c, y)) for k in range(3)]
-
-    def spread_own(j):
-        a = pass_on(block(line[j], x, y, 0), gxa, j, to_x)
-        b = pass_on(block(line[j], x, y, 1), gyb, j, to_y)
-        pass_on(block(line[j], x, y, 0), gya, j, to_y)
-        pass_on(block(line[j], x, y, 1), gxb, j, to_x)
-        pass_on(block(line[j], x, y), gc, j, to_c)
-        return a, b
-
-    own = [spread_own(0)]
+    zc = [
+        [pass_on(block(g, z, x, y), gz, g * 3 + k, device(line[k + 1], x, c, y)) for k in range(3)]
+        for g in (0, 1)
+    ]
+    own = {}
+
+    def spread_own(g, j):
+        a = pass_on(block(g, line[j], x, y, 0), gxa, g * 4 + j, to_x)
+        b = pass_on(block(g, line[j], x, y, 1), gyb, g * 4 + j, to_y)
+        pass_on(block(g, line[j], x, y, 0), gya, g * 8 + j, to_y)
+        pass_on(block(g, line[j], x, y, 1), gxb, g * 8 + j, to_x)
+        pass_on(block(g, line[j], x, y), gc, g * 28 + j, to_c)
+        own[g, j] = a, b
+
+    spread_own(0, 0)
 
     number = lax.broadcasted_iota(jnp.int32, (16, sets), 1) + 1
     first = lax.broadcasted_iota(jnp.int32, (16, sets), 0) == 0
@@ -157,61 +173,85 @@
                 to = ((p // 2) % 2 * 4 + p // 4) * rows
                 bt_ref[p % 2, to : to + rows, :] = part[n * rows : (n + 1) * rows, :]
 
-    def spread_far(j):
-        own[j][0].wait_recv()
-        pass_on(block(line[j], 1 - x, y, 0), gya, 4 + j, to_y)
-        pass_on(block(line[j], 1 - x, y, 0), gc, 4 + j, to_c)
-        own[j][1].wait_recv()
-        pass_on(block(line[j], x, 1 - y, 1), gxb, 4 + j, to_x)
-        pass_on(block(line[j], x, 1 - y, 1), gc, 8 + j, to_c)
+    def spread_far(g, j):
+        own[g, j][0].wait_recv()
+        pass_on(block(g, line[j], 1 - x, y, 0), gya, g * 8 + 4 + j, to_y)
+        pass_on(block(g, line[j], 1 - x, y, 0), gc, g * 28 + 4 + j, to_c)
+        own[g, j][1].wait_recv()
+        pass_on(block(g, line[j], x, 1 - y, 1), gxb, g * 8 + 4 + j, to_x)
+        pass_on(block(g, line[j], x, 1 - y, 1), gc, g * 28 + 8 + j, to_c)
+
+    def landed(part, sems, i):
+        remote(part, part, sems, i, to_c).wait_recv()
+        return part
+
+    def from_core(g, numbers):
+        for i in numbers:
+            landed(block(g, z, x, y) if i < 4 else block(g, z, x, y, 0), gc, g * 28 + i)
+
+    def to_core(g):
+        for j in range(4):
+            pass_on(landed(block(g, line[j], 1 - x, y, 1), gxb, g * 8 + j), gc, g * 28 + 16 + j, to_c)
+            pass_on(landed(block(g, line[j], x, 1 - y, 0), gya, g * 8 + j), gc, g * 28 + 12 + j, to_c)
+
+    def far(g, j):
+        pass_on(landed(block(g, line[j], 1 - x, 1 - y, 0), gya, g * 8 + 4 + j), gc, g * 28 + 20 + j, to_c)
+        pass_on(landed(block(g, line[j], 1 - x, 1 - y, 1), gxb, g * 8 + 4 + j), gc, g * 28 + 24 + j, to_c)
+
+    near_core = [0, 1, 2, 3, 4, 5, 6, 7, 16, 17, 18, 19]
+    far_core = [8, 9, 10, 11, 12, 13, 14, 15, 20, 21, 22, 23, 24, 25, 26, 27]
 
     netted[...] = jnp.zeros_like(netted)
-    zc[0].wait_recv()
-    own.append(spread_own(1))
+    zc[0][0].wait_recv()
+    spread_own(0, 1)
     fetch.wait()
     lax.fori_loop(0, cols // 512, find, 0)
     idx_copy = pass_on(idxo.at[y], gi, 0, to_y)
-    spread_far(0)
-    build(y)
-    zc[1].wait_recv()
-    own.append(spread_own(2))
-    spread_far(1)
+    spread_far(0, 0)
+    zc[0][1].wait_recv()
+    spread_own(0, 2)
+    spread_far(0, 1)
+    spread_own(1, 0)
     fetch_half.wait()
     turn()
+    zc[0][2].wait_recv()
+    spread_own(0, 3)
+    spread_far(0, 2)
+    build(y)
+    spread_far(0, 3)
+    to_core(0)
+    zc[1][0].wait_recv()
+    spread_own(1, 1)
+    spread_far(1, 0)
+    for j in range(4):
+        far(0, j)
+    zc[1][1].wait_recv()
+    spread_own(1, 2)
+    spread_far(1, 1)
+    from_core(0, near_core)
+    forward(y, 0, 1)
+    zc[1][2].wait_recv()
+    spread_own(1, 3)
+    spread_far(1, 2)
     idx_copy.wait_recv()
     build(1 - y)
-    zc[2].wait_recv()
-    own.append(spread_own(3))
-    spread_far(2)
-    spread_far(3)
-
-    def landed(part, sems, i):
-        remote(part, part, sems, i, to_c).wait_recv()
-        return part
-
-    def from_core(numbers):
-        for i in numbers:
-            landed(block(z, x, y) if i < 4 else block(z, x, y, 0), gc, i)
-
-    for j in range(4):
-        pass_on(landed(block(line[j], 1 - x, y, 1), gxb, j), gc, 16 + j, to_c)
-    for j in range(4):
-        pass_on(landed(block(line[j], x, 1 - y, 0), gya, j), gc, 12 + j, to_c)
-    from_core([0, 1, 2, 3, 4, 5, 6, 7, 16, 17, 18, 19])
-    forward(y, 0, 2)
-
-    def far(j):
-        pass_on(landed(block(line[j], 1 - x, 1 - y, 0), gya, 4 + j), gc, 20 + j, to_c)
-        pass_on(landed(block(line[j], 1 - x, 1 - y, 1), gxb, 4 + j), gc, 24 + j, to_c)
-
-    far(0)
-    far(1)
-    far(2)
-    far(3)
+    spread_far(1, 3)
+    forward(y, 1, 2)
+    to_core(1)
+    from_core(0, far_core)
+    forward(1 - y, 0, 1)
+    far(1, 0)
+    far(1, 1)
+    forward(1 - y, 1, 2)
+    far(1, 2)
+    far(1, 3)
+    from_core(1, near_core)
     forward(y, 2, 4)
-    from_core([8, 9, 10, 11, 12, 13, 14, 15, 20, 21, 22, 23, 24, 25, 26, 27])
-    forward(1 - y, 0, 4)
-
+    from_core(1, far_core)
+    forward(1 - y, 2, 4)
+
+    for copy in small:
+        copy.wait()
     scale, borrow, lend = lax.rsqrt(counts_ref[...].astype(f32)), borrow_ref[...], lend_ref[...]
 
     def fund(r, carry):
@@ -347,7 +387,7 @@
     steps = 4
     width, side = cols // 2 // steps, rows * 4
     buffers = [
-        ((trades, sets), membership.dtype), ((paths, k), b), ((2, 8 * rows, paths), b), ((k, 2 * cols), b), ((2, 8, cols), f), ((sets, 2 * cols), b),
+        ((1, sets), counts.dtype), ((1, sets), f), ((1, sets), f), ((trades, sets), membership.dtype), ((paths, k), b), ((2, 8 * rows, paths), b), ((k, 2 * cols), b), ((2, 8, cols), f), ((sets, 2 * cols), b),
         ((paths, 2 * cols), f), ((paths, 512), b), ((paths, sets), f), ((paths, sets), b), ((paths, 2 * cols), b),
         ((4 * steps, 2 * side, width), b), ((4 * steps, 2 * side, width), b), ((4 * steps, 2 * side, width), f),
         ((steps, 2 * side, width), b), ((steps, 2 * side, width), b),
@@ -356,16 +396,16 @@
         ((steps, side, width), b), ((steps, side, width), b),
         ((2 * steps, side, width), b), ((6 * steps, rows, width), b),
     ]
-    lengths = (3, 4, 8, 8, 4, 28, 1, 4 * steps, steps, steps, 2 * steps, steps, 6 * steps)
+    lengths = (6, 8, 16, 16, 8, 56, 1, 4 * steps, steps, steps, 2 * steps, steps, 6 * steps)
     sems = [pltpu.SemaphoreType.DMA((n,)) for n in lengths for _ in range(2)]
     return pl.pallas_call(
         adjoint_kernel,
         out_shape=(jax.ShapeDtypeStruct((2, paths, k), f), jax.ShapeDtypeStruct((rows, cols), f)),
-        in_specs=[pl.BlockSpec(memory_space=pl.ANY)] * 2 + [VMEM] * 4,
+        in_specs=[pl.BlockSpec(memory_space=pltpu.HBM)] * 6,
         out_specs=(VMEM, VMEM),
-        scratch_shapes=[pltpu.VMEM(shape, kind) for shape, kind in buffers] + [pltpu.SemaphoreType.DMA] * 2 + sems,
+        scratch_shapes=[pltpu.VMEM(shape, kind) for shape, kind in buffers] + [pltpu.SemaphoreType.DMA((6,))] + sems,
         compiler_params=pltpu.CompilerParams(
-            collective_id=0, has_side_effects=True, vmem_limit_bytes=50 * 1024 * 1024
+            collective_id=0, has_side_effects=True, vmem_limit_bytes=56 * 1024 * 1024
         ),
         name="adjoint",
     )(membership, basis, coef, counts, borrow, lend)

time: 83.3 us -> 83.1 us (level)
  local copies, waits for them, and re-layouts: 4.16 us -> 0.01 us
  Pallas kernels: 76.3 us -> 78.8 us
  other arithmetic: 1.9 us -> 3.48 us
    unnamed x10 -> x2, local copies, waits for them, and re-layouts: 4.16 us -> 0.01 us
    pallas_call x1, Pallas kernels: 76.3 us -> 78.8 us  [adjoint(): pl.pallas_call(adjoint_kernel, out_shape=(jax.ShapeDtypeStruct((2, paths,...]
    add x1, other arithmetic: 1.18 us -> 2.76 us  [body(): return (parts[0] + parts[1], total * factor)]
where the time goes in v4:
time: 83.1 us; the launch traced here: 83 us
  Pallas kernels  78.8 us (95%)
  other arithmetic  3.48 us (4%)
    pallas_call x1, Pallas kernels, adjoint(): pl.pallas_call(adjoint_kernel, out_shape=(jax.ShapeDtypeStruct((2, paths,...  78.8 us
    add x1, other arithmetic, body(): return (parts[0] + parts[1], total * factor)  2.76 us

profile of v4, /device:TPU:0, one launch (start us, length us, event | category | flops | bytes accessed | tf_op | source)
XLA Modules:
  0.0 83.0 jit_solution(7306460900752174679)
XLA Ops:
  0.6 78.8 %adjoint.1 = (f32[2,512,512]{2,1,0:T(8,128)}, f32[32,2048]{1,0:T(8,128)}) custom-call(s32[2048,512]{1,0:T(8,128)} %member_ref.1, bf16[1024,512]{1,0:T(8,128)(2,1)} %basis_ref.1, bf16[32,2048]{1,0:T(8,128)(2,1)} %coef_ref.1, s32[1,512]{1,0:T(1,128)} %bitcast.5, f32[1,512]{1,0:T(1,128)} %bitcast.6, f32[1,512]{1,0:T(1,128)} %bitcast.7), custom_call_target="tpu_custom_call" | custom-call | tf_op jit(solution)/shard_map/adjoint/pallas_call | solution.py:401
  79.5 0.0 copy-start
  79.5 2.8 %add_bitcast_fusion = f32[512,512]{1,0:T(8,128)} fusion(f32[2,512,512]{2,1,0:T(8,128)} %get-tuple-element.4), kind=kLoop, calls=%fused_computation | loop fusion | flops 262144 | bytes 3145728 | tf_op jit(solution)/shard_map/add | solution.py:426
  82.2 0.0 copy-done
  82.2 0.7 broadcast_multiply_fusion
Async XLA Ops:
  79.5 2.8 %copy-start = (f32[32,2048]{1,0:T(8,128)S(1)}, f32[32,2048]{1,0:T(8,128)}, u32[]{:S(2)}) copy-start(f32[32,2048]{1,0:T(8,128)} %get-tuple-element.5) | copy-start | bytes 786436

commit v5 on v4

--- a/solution.py
+++ b/solution.py
@@ -1,3 +1,5 @@
+import functools
+
 import jax
 import jax.numpy as jnp
 from jax import lax
@@ -229,20 +231,18 @@
     spread_own(1, 2)
     spread_far(1, 1)
     from_core(0, near_core)
-    forward(y, 0, 1)
     zc[1][2].wait_recv()
     spread_own(1, 3)
     spread_far(1, 2)
     idx_copy.wait_recv()
     build(1 - y)
     spread_far(1, 3)
-    forward(y, 1, 2)
+    forward(y, 0, 2)
     to_core(1)
     from_core(0, far_core)
-    forward(1 - y, 0, 1)
     far(1, 0)
     far(1, 1)
-    forward(1 - y, 1, 2)
+    forward(1 - y, 0, 2)
     far(1, 2)
     far(1, 3)
     from_core(1, near_core)
@@ -268,7 +268,6 @@
     width = half // steps
     side = rows * 4
     mine, theirs = pl.ds(pl.multiple_of(x * side, side), side), pl.ds(pl.multiple_of((1 - x) * side, side), side)
-    copies = {}
 
     def columns(s, i):
         q = i // 2
@@ -301,72 +300,76 @@
 
         lax.fori_loop(0, 4, chunk, 0)
         yso[s] = acc[s * 4].astype(bf16)
-        copies["ya", s] = send(yso.at[s], yri.at[s], yas, s, to_y)
+        ya_copy(s).start()
         for q in (0, 1):
             j = q * steps + s
             xbo[j] = acc[s * 4 + 1 + q, theirs].astype(bf16)
-            copies["xb", j] = send(xbo.at[j], xbi.at[j], xbs, j, to_x)
+            xb_copy(j).start()
+
+    def ya_copy(s):
+        return remote(yso.at[s], yri.at[s], yas, s, to_y)
+
+    def xb_copy(j):
+        return remote(xbo.at[j], xbi.at[j], xbs, j, to_x)
+
+    def yb_copy(s):
+        return remote(ybo.at[s], ybi.at[s], ybs, s, to_y)
+
+    def xa_copy(s):
+        return remote(xso.at[s], xri.at[s], xas, s, to_x)
+
+    def z_copy(k, j):
+        zk = line[k + 1]
+        part = zso.at[j, pl.ds(pl.multiple_of(zk * rows, rows), rows)]
+        n = k * 2 * steps + j
+        return remote(part, zri.at[n], zs, n, device(zk, x, c, y))
 
     def third_step(s):
-        copies["xb", s].wait_recv()
+        xb_copy(s).wait_recv()
         ybo[s] = (acc[s * 4 + 1, mine] + xbi[s].astype(f32)).astype(bf16)
-        copies["yb", s] = send(ybo.at[s], ybi.at[s], ybs, s, to_y)
-        copies["ya", s].wait_recv()
+        yb_copy(s).start()
+        ya_copy(s).wait_recv()
         xso[s] = (acc[s * 4 + 3, theirs] + yri[s, theirs].astype(f32)).astype(bf16)
-        copies["xa", s] = send(xso.at[s], xri.at[s], xas, s, to_x)
+        xa_copy(s).start()
         acc[s * 4 + 3, mine] = acc[s * 4 + 3, mine] + yri[s, mine].astype(f32)
-        copies["xb", steps + s].wait_recv()
+        xb_copy(steps + s).wait_recv()
         acc[s * 4 + 2, mine] = acc[s * 4 + 2, mine] + xbi[steps + s].astype(f32)
 
     def fourth_step(s):
         for h in (1, 0):
             i, j = s * 4 + (2 if h else 3), h * steps + s
-            copies["yb" if h else "xa", s].wait_recv()
+            (yb_copy(s) if h else xa_copy(s)).wait_recv()
             arrived = ybi[s] if h else xri[s]
             acc[i, mine] = acc[i, mine] + arrived.astype(f32)
             zso[j] = acc[i, mine].astype(bf16)
             for k in range(3):
-                zk = line[k + 1]
-                part = zso.at[j, pl.ds(pl.multiple_of(zk * rows, rows), rows)]
-                n = k * 2 * steps + j
-                copies["z", n] = send(part, zri.at[n], zs, n, device(zk, x, c, y))
+                z_copy(k, j).start()
 
     def last_step(s):
         for h in (1, 0):
             i, j = s * 4 + (2 if h else 3), h * steps + s
             total = acc[i, pl.ds(pl.multiple_of(x * side + z * rows, rows), rows)]
             for k in range(3):
-                copies["z", k * 2 * steps + j].wait_recv()
+                z_copy(k, j).wait_recv()
                 total = total + zri[k * 2 * steps + j].astype(f32)
             out_ref[:, pl.ds(j * width, width)] = total
 
-    def basis_part(n, k):
+    def basis_part(i):
+        n, k = i // 2, lax.rem(i, 2)
         size = full_ref.shape[0] // 2
-        to, over = slice(k * size, (k + 1) * size), slice(n * cols, (n + 1) * cols)
+        to = pl.ds(pl.multiple_of(k * size, size), size)
+        over = pl.ds(pl.multiple_of(n * cols, cols), cols)
         db_ref[n, :, to] = lax.dot_general(
             vg[:, over], full_ref[to, over], NT, preferred_element_type=f32
         )
 
-    first_step(0)
-    first_step(1)
-    second_step(0)
-    first_step(2)
-    second_step(1)
-    third_step(0)
-    first_step(3)
-    second_step(2)
-    fourth_step(0)
-    third_step(1)
-    second_step(3)
-    basis_part(0, 0)
-    third_step(2)
-    fourth_step(1)
-    basis_part(0, 1)
-    third_step(3)
-    fourth_step(2)
-    basis_part(1, 0)
-    fourth_step(3)
-    basis_part(1, 1)
+    def stage(m, carry):
+        for lag, step in enumerate((first_step, second_step, third_step, fourth_step)):
+            pl.when((m >= lag) & (m < lag + steps))(functools.partial(step, m - lag))
+        pl.when(m >= 3)(functools.partial(basis_part, m - 3))
+        return carry
+
+    lax.fori_loop(0, steps + 3, stage, 0)
     for s in range(steps):
         last_step(s)
 
@@ -375,6 +378,16 @@
         return carry
 
     lax.fori_loop(0, 4 * steps, sent, 0)
+
+    def sent_later(s, carry):
+        for copy in (ya_copy(s), xa_copy(s), yb_copy(s), xb_copy(s), xb_copy(steps + s)):
+            copy.wait_send()
+        for k in range(3):
+            z_copy(k, s).wait_send()
+            z_copy(k, steps + s).wait_send()
+        return carry
+
+    lax.fori_loop(0, steps, sent_later, 0)
     for copy in started:
         copy.wait_send()
 

time: 83.1 us -> 83.8 us (level)
  no operation moved by 1% of the time
where the time goes in v5:
time: 83.8 us; the launch traced here: 83.7 us
  Pallas kernels  79.5 us (95%)
  other arithmetic  3.48 us (4%)
    pallas_call x1, Pallas kernels, adjoint(): pl.pallas_call(adjoint_kernel, out_shape=(jax.ShapeDtypeStruct((2, paths,...  79.5 us
    add x1, other arithmetic, body(): return (parts[0] + parts[1], total * factor)  2.76 us

profile of v5, /device:TPU:0, one launch (start us, length us, event | category | flops | bytes accessed | tf_op | source)
XLA Modules:
  0.0 83.7 jit_solution(1001131333133224605)
XLA Ops:
  0.6 79.5 %adjoint.1 = (f32[2,512,512]{2,1,0:T(8,128)}, f32[32,2048]{1,0:T(8,128)}) custom-call(s32[2048,512]{1,0:T(8,128)} %member_ref.1, bf16[1024,512]{1,0:T(8,128)(2,1)} %basis_ref.1, bf16[32,2048]{1,0:T(8,128)(2,1)} %coef_ref.1, s32[1,512]{1,0:T(1,128)} %bitcast.5, f32[1,512]{1,0:T(1,128)} %bitcast.6, f32[1,512]{1,0:T(1,128)} %bitcast.7), custom_call_target="tpu_custom_call" | custom-call | tf_op jit(solution)/shard_map/adjoint/pallas_call | solution.py:414
  80.2 0.0 copy-start
  80.2 2.8 %add_bitcast_fusion = f32[512,512]{1,0:T(8,128)} fusion(f32[2,512,512]{2,1,0:T(8,128)} %get-tuple-element.4), kind=kLoop, calls=%fused_computation | loop fusion | flops 262144 | bytes 3145728 | tf_op jit(solution)/shard_map/add | solution.py:439
  83.0 0.0 copy-done
  83.0 0.7 broadcast_multiply_fusion
Async XLA Ops:
  80.2 2.8 %copy-start = (f32[32,2048]{1,0:T(8,128)S(1)}, f32[32,2048]{1,0:T(8,128)}, u32[]{:S(2)}) copy-start(f32[32,2048]{1,0:T(8,128)} %get-tuple-element.5) | copy-start | bytes 786436
